TPU v7x, 32 devices: a whole 2x2x4 slice. The times are simulated.
32 devices in a mesh: grp: 2 (over y), ae: 4 (over z), tp: 2 (over x), sub: 2 (over core).
Axes of the slice: x: 2, y: 2, z: 4, core: 2. Of those that a mesh axis runs over, the one named last changes fastest.
Arguments:
- tokens: bfloat16 [256, 3072], P(('grp', 'ae', 'sub'), 'tp'), parts along dimension 0
- queries: bfloat16 [256, 3072], P(('grp', 'ae', 'sub'), 'tp'), parts along dimension 0, may hold values from -2 to 2
- kv_cache: bfloat16 [2, 256, 8, 64, 128], P(None, ('grp', 'ae', 'sub'), 'tp'), parts along dimension 1, may hold values from -2 to 2
- new_kv: bfloat16 [2, 256, 1024], P(None, ('grp', 'ae', 'sub'), 'tp'), parts along dimension 1, may hold values from -2 to 2
- lengths: int32 [256], P(('grp', 'ae', 'sub')), parts along dimension 0, may hold values from 1 to 64
- routes: int32 [256, 4], P(('grp', 'ae', 'sub')), parts along dimension 0, may hold values from 0 to 15, all different within a row; in each aligned block of 16 rows (0 to 15, 16 to 31, ...) at most 5 rows name the same one
- placement: int32 [16], replicated, may hold values from 0 to 15, each once
- router_weight: bfloat16 [3072, 16], replicated, may hold values from -0.109375 to 0.109375
- w_up: bfloat16 [16, 3072, 5376], P('ae', None, ('tp', 'sub')), may hold values from -0.109375 to 0.109375
- w_down: bfloat16 [16, 5376, 3072], P('ae', ('tp', 'sub')), may hold values from -0.109375 to 0.109375
Outputs:
- expert_mix: bfloat16 [256, 3072], P(('grp', 'ae', 'sub'), 'tp'), parts along dimension 0
There are 2 independent parts, one for each index of `grp`. A program takes and returns all parts, laid end to end along the dimension named above; an argument that names none is the same for every part. Nothing has to cross between parts.
Inputs may be any that keep to these rules, and one draw needn't show every extreme that they name: `routes`: each row names 4 different experts. In each aligned block of 16 rows (the rows of one device) no expert is named by more than 5 rows, and in some block one expert is named by exactly 5 rows. A permutation: expert e uses entry placement[e] of w_up and w_down.
All inputs are finite; a program needn't handle non-finite values.
Results may differ from a plain program's by a relative error of at most 0.0085.
Values may be sent and summed in bfloat16 or wider, within the bound.
No kernel may reach another device: no remote copies, remote signals or barrier semaphores. Data moves between devices by JAX's collectives and lax.ppermute only.
A program may use at most 256 MiB of HBM per device.

v0:
```python
import math

import jax
import jax.numpy as jnp
from jax import lax
from jax.sharding import PartitionSpec as P

CAP = 5


EPSILON = 1e-05


def per_device(
    tokens, queries, kv_cache, new_kv, lengths, routes, placement, router_weight, w_up, w_down
):
    row_count, slice_width = tokens.shape
    local_heads = kv_cache.shape[2]
    context = kv_cache.shape[3]
    head_width = kv_cache.shape[4]
    per_key = slice_width // (local_heads * head_width)
    score_scale = 1.0 / math.sqrt(head_width)
    query_heads = queries.reshape(row_count, local_heads, per_key, head_width)
    scores = (
        jnp.einsum("rgqd,rgjd->rgqj", query_heads, kv_cache[0], preferred_element_type=jnp.float32)
        * score_scale
    )
    fresh_key = new_kv[0].reshape(row_count, local_heads, head_width)
    fresh_value = new_kv[1].reshape(row_count, local_heads, head_width)
    own_score = (
        jnp.einsum("rgqd,rgd->rgq", query_heads, fresh_key, preferred_element_type=jnp.float32)
        * score_scale
    )
    visible = (
        jnp.arange(context, dtype=jnp.int32)[None, None, None, :] < lengths[:, None, None, None]
    )
    weights = jnp.where(visible, jnp.exp(scores), 0.0)
    own_weight = jnp.exp(own_score)
    denominator = jnp.sum(weights, -1) + own_weight
    attention_probs = (weights / denominator[..., None]).astype(jnp.bfloat16)
    own_prob = (own_weight / denominator).astype(jnp.bfloat16)
    attended = jnp.einsum(
        "rgqj,rgjd->rgqd", attention_probs, kv_cache[1], preferred_element_type=jnp.float32
    )
    attended = (
        attended
        + own_prob.astype(jnp.float32)[..., None] * fresh_value.astype(jnp.float32)[:, :, None, :]
    )
    hidden_state = (tokens.astype(jnp.float32) + attended.reshape(row_count, slice_width)).astype(
        jnp.bfloat16
    )
    model_width = router_weight.shape[0]
    experts = router_weight.shape[1]
    full_state = lax.all_gather(hidden_state, "tp", axis=1, tiled=True)
    wide_full = full_state.astype(jnp.float32)
    square_sum = jnp.sum(wide_full * wide_full, -1)
    raw_logits = jnp.dot(full_state, router_weight, preferred_element_type=jnp.float32)
    inverse = lax.rsqrt(square_sum / model_width + EPSILON)
    logits = raw_logits * inverse[:, None]
    normed = (hidden_state.astype(jnp.float32) * inverse[:, None]).astype(jnp.bfloat16)
    picks = routes.shape[1]
    expert_ids = jnp.arange(experts, dtype=jnp.int32)
    picked_mask = (routes[:, :, None] == expert_ids[None, None, :]).astype(jnp.float32)
    chosen = jnp.sum(picked_mask * logits[:, None, :], -1)
    gate_exp = jnp.exp(chosen)
    gate_values = gate_exp / jnp.sum(gate_exp, -1, keepdims=True)
    flat_onehot = (routes.reshape(-1)[:, None] == expert_ids[None, :]).astype(jnp.int32)
    earlier = jnp.cumsum(flat_onehot, 0) - flat_onehot
    position = jnp.sum(flat_onehot * earlier, -1)
    slot_index = jnp.sum(flat_onehot * placement[None, :], -1)
    column = slot_index * CAP + position
    slot_total = experts * CAP
    match = jnp.sum(
        (
            column.reshape(row_count, picks)[:, :, None]
            == jnp.arange(slot_total, dtype=jnp.int32)[None, None, :]
        ).astype(jnp.int32),
        1,
    ).astype(jnp.bfloat16)
    packed = jnp.einsum("rc,rd->cd", match, normed, preferred_element_type=jnp.float32).astype(
        jnp.bfloat16
    )
    owners = lax.axis_size("ae")
    local_experts = w_up.shape[0]
    outgoing = packed.reshape(owners, local_experts, CAP, slice_width)
    arrived = lax.all_to_all(outgoing, "ae", split_axis=0, concat_axis=0, tiled=True)
    arrived = lax.all_gather(arrived, "sub", axis=0, tiled=True)
    up_parts = (w_up,)
    down_parts = (w_down,)
    column_piece = lax.all_gather(arrived, "tp", axis=3, tiled=True)
    up_sums = tuple(
        (
            jnp.einsum("nlcd,ldf->nlcf", column_piece, up_part, preferred_element_type=jnp.float32)
            for up_part in up_parts
        )
    )
    heads_axis = lax.axis_size("tp")
    term = None
    for up_total, down_part in zip(up_sums, down_parts):
        expert_hidden = jax.nn.silu(up_total).astype(jnp.bfloat16)
        shaped_down = down_part.reshape(local_experts, down_part.shape[1], heads_axis, slice_width)
        piece_term = jnp.einsum(
            "nlcf,lftd->tnlcd", expert_hidden, shaped_down, preferred_element_type=jnp.float32
        )
        term = piece_term
    term = term.reshape(-1, slice_width)
    summed = lax.psum_scatter(term, ("tp", "sub"), scatter_dimension=0, tiled=True)
    expert_output = summed.astype(jnp.bfloat16).reshape(owners, local_experts * CAP, slice_width)
    returned = lax.all_to_all(expert_output, "ae", split_axis=0, concat_axis=0, tiled=True).reshape(
        slot_total, slice_width
    )
    picked_rows = jnp.take(returned, column, axis=0).reshape(row_count, picks, slice_width)
    expert_mix = jnp.sum(gate_values[:, :, None] * picked_rows.astype(jnp.float32), 1)
    return expert_mix.astype(jnp.bfloat16)


def solution(mesh):
    placed = (
        P(("grp", "ae", "sub"), "tp"),
        P(("grp", "ae", "sub"), "tp"),
        P(None, ("grp", "ae", "sub"), "tp", None, None),
        P(None, ("grp", "ae", "sub"), "tp"),
        P(("grp", "ae", "sub")),
        P(("grp", "ae", "sub"), None),
        P(),
        P(),
        P("ae", None, ("tp", "sub")),
        P("ae", ("tp", "sub"), None),
    )
    return jax.shard_map(
        per_device,
        mesh=mesh,
        in_specs=placed,
        out_specs=P(("grp", "ae", "sub"), "tp"),
        check_vma=False,
    )
```

profile of v0, /device:TPU:0, one launch (start us, length us, event | category | flops | bytes accessed | tf_op | source)
XLA Modules:
  0.0 213.8 jit_solution(3743848690929297799)
XLA Ops:
  6.5 0.8 iota_compare_fusion.3
  7.3 0.8 copy.33
  8.3 0.8 select_reduce_fusion.1
  9.4 0.7 fusion.28
  10.2 0.8 reshape.132
  11.3 2.0 fusion.29
  13.3 1.7 convolution_add_fusion
  15.0 0.8 add_convert_fusion
  15.8 5.7 %all_gather.9 = bf16[16,3072]{1,0:T(8,128)(2,1)S(1)} all-gather(bf16[16,1536]{1,0:T(8,128)(2,1)S(1)} %add_convert_fusion), channel_id=1, replica_groups=mesh['grp'=2,'ae'=4,'tp'=2,'sub'=2] {'tp'}, dimensions={1}, use_global_device_ids=true | all-gather | bytes 147456 | tf_op jit(solution)/shard_map/all_gather | solution.py:54
  22.0 0.8 copy.35
  22.9 5.4 %all-to-all-start = ((bf16[4,4,5,1536]{3,1,2,0:T(4,128)(2,1)}), bf16[4,4,5,1536]{3,1,2,0:T(4,128)(2,1)S(1)}, u32[]{:S(2)}, u32[]{:S(2)}) async-start(bf16[4,4,5,1536]{3,1,2,0:T(4,128)(2,1)} %copy.35), calls=%async_computation | async-start | bytes 491520 | tf_op jit(solution)/shard_map/all_to_all | solution.py:86
  28.3 71.8 %reshape.135 = bf16[4,1344,2,1536]{3,2,1,0:T(2,128)(2,1)} reshape(bf16[4,1344,3072]{2,1,0:T(8,128)(2,1)} %param.19) | data formatting | bytes 66060288 | tf_op jit(solution)/shard_map/reshape | solution.py:101
  100.1 2.1 %all_gather.10 = bf16[8,4,5,1536]{3,1,2,0:T(4,128)(2,1)S(1)} all-gather(bf16[4,4,5,1536]{3,1,2,0:T(4,128)(2,1)S(1)} %all-to-all-done), channel_id=1, replica_groups=mesh['grp'=2,'ae'=4,'tp'=2,'sub'=2] {'sub'}, dimensions={0}, use_global_device_ids=true | all-gather | bytes 737280 | tf_op jit(solution)/shard_map/all_gather | solution.py:87
  102.4 14.1 %all_gather.11 = bf16[8,4,5,3072]{3,0,2,1:T(8,128)(2,1)S(1)} all-gather(bf16[8,4,5,1536]{3,0,2,1:T(8,128)(2,1)S(1)} %copy.36), channel_id=1, replica_groups=mesh['grp'=2,'ae'=4,'tp'=2,'sub'=2] {'tp'}, dimensions={3}, use_global_device_ids=true | all-gather | bytes 1474560 | tf_op jit(solution)/shard_map/all_gather | solution.py:90
  116.5 15.1 %fusion.18 = bf16[8,4,5,1344,1]{3,0,4,2,1:T(8,128)(2,1)S(1)} fusion(bf16[8,4,5,3072]{3,0,2,1:T(8,128)(2,1)S(1)} %all_gather.11, bf16[4,3072,1344]{1,2,0:T(8,128)(2,1)} %param.18), kind=kOutput, calls=%fused_computation.18 | convolution fusion | flops 1322280960 | bytes 34443264 | tf_op jit(solution)/shard_map/nlcd,ldf->nlcf/dot_general | solution.py:93
  131.6 20.9 %fusion.4 = f32[2,8,4,5,1536]{4,1,0,3,2:T(8,128)} fusion(bf16[8,4,5,1344,1]{3,0,4,2,1:T(8,128)(2,1)S(1)} %fusion.18, bf16[4,1344,2,1536,1]{3,2,1,0,4:T(2,128)(2,1)} %bitcast.45), kind=kOutput, calls=%fused_computation.5 | convolution fusion | flops 1321205760 | bytes 35426304 | tf_op jit(solution)/shard_map/nlcf,lftd->tnlcd/dot_general | solution.py:102
  152.4 2.8 %copy.38 = f32[2,8,4,5,1536]{4,3,2,1,0:T(8,128)S(1)} copy(f32[2,8,4,5,1536]{4,1,0,3,2:T(8,128)} %fusion.4) | data formatting | bytes 3932160 | tf_op jit(solution)/shard_map/nlcf,lftd->tnlcd/transpose | solution.py:102
  155.2 1.5 reshape.136
  157.1 31.9 %reduce-scatter.2.cloned.1.call-done = f32[80,1536]{1,0:T(8,128)} async-done(((f32[320,1536]{1,0:T(8,128)}), f32[80,1536]{1,0:T(8,128)}) %reduce-scatter.2.cloned.1.call-update) | async-done | bytes 491536 | tf_op jit(solution)/shard_map/reduce_scatter | solution.py:107
  189.0 1.1 convert_element_type.74
  190.0 0.8 reshape.137
  190.8 4.6 %all-to-all-start.1 = ((bf16[4,20,1536]{2,1,0:T(8,128)(2,1)}), bf16[4,20,1536]{2,1,0:T(8,128)(2,1)S(1)}, u32[]{:S(2)}, u32[]{:S(2)}) async-start(bf16[4,20,1536]{2,1,0:T(8,128)(2,1)} %reshape.137), calls=%async_computation.2 | async-start | bytes 589824 | tf_op jit(solution)/shard_map/all_to_all | solution.py:109
  195.5 9.5 %all-to-all-done.1 = bf16[4,20,1536]{2,1,0:T(8,128)(2,1)S(1)} async-done(((bf16[4,20,1536]{2,1,0:T(8,128)(2,1)}), bf16[4,20,1536]{2,1,0:T(8,128)(2,1)S(1)}, u32[]{:S(2)}, u32[]{:S(2)}) %all-to-all-start.1) | async-done | bytes 245792 | tf_op jit(solution)/shard_map/all_to_all | solution.py:109
  205.8 1.1 multiply_reduce_fusion
  (34 shorter events, 2.7 us)
Async XLA Ops:
  6.5 150.2 %copy-start = (bf16[3072,16]{0,1:T(8,128)(2,1)S(1)}, bf16[3072,16]{0,1:T(8,128)(2,1)}, u32[]{:S(2)}) copy-start(bf16[3072,16]{0,1:T(8,128)(2,1)} %param.17) | copy-start | bytes 294916
  22.9 77.2 %all-to-all-start = ((bf16[4,4,5,1536]{3,1,2,0:T(4,128)(2,1)}), bf16[4,4,5,1536]{3,1,2,0:T(4,128)(2,1)S(1)}, u32[]{:S(2)}, u32[]{:S(2)}) async-start(bf16[4,4,5,1536]{3,1,2,0:T(4,128)(2,1)} %copy.35), calls=%async_computation | async-start | bytes 491520 | tf_op jit(solution)/shard_map/all_to_all | solution.py:86
  28.3 160.6 %reduce-scatter.2.cloned.1.call-start = ((), (), s32[]{:S(2)}) async-start(), calls=%async_computation.3 | async-start | bytes 2457600 | tf_op jit(solution)/shard_map/reduce_scatter | solution.py:107
  131.6 25.3 %copy-start.1 = (s32[16,4]{0,1:T(4,128)S(1)}, s32[16,4]{0,1:T(4,128)}, u32[]{:S(2)}) copy-start(s32[16,4]{0,1:T(4,128)} %param.15) | copy-start | bytes 772
  190.8 14.2 %all-to-all-start.1 = ((bf16[4,20,1536]{2,1,0:T(8,128)(2,1)}), bf16[4,20,1536]{2,1,0:T(8,128)(2,1)S(1)}, u32[]{:S(2)}, u32[]{:S(2)}) async-start(bf16[4,20,1536]{2,1,0:T(8,128)(2,1)} %reshape.137), calls=%async_computation.2 | async-start | bytes 589824 | tf_op jit(solution)/shard_map/all_to_all | solution.py:109
Sparse Core Ops, SparseCore 0:
  156.8 32.0 reduce-scatter.1
where the time goes:
time: 216 us; the launch traced here: 214 us
  local copies, waits for them, and re-layouts  80.7 us (37%)
  waiting for transfers between devices  41.4 us (19%)
  matrix products  40.2 us (19%)
  blocking collectives  21.9 us (10%)
  between operations  13.5 us (6%)
  starting transfers between devices  10 us (5%)
  other arithmetic  5.99 us (3%)
    reshape x1, local copies, waits for them, and re-layouts, per_device(): down_part.reshape(local_experts, down_part.shape[1], heads_axis, slice_wi...  71.8 us
    reduce_scatter x1, waiting for transfers between devices, per_device(): lax.psum_scatter(term, ('tp', 'sub'), scatter_dimension=0, tiled=True)  31.9 us
    dot_general x1, matrix products, per_device(): jnp.einsum('nlcf,lftd->tnlcd', expert_hidden, shaped_down, preferred_elem...  20.9 us
    dot_general x1, matrix products, per_device(): jnp.einsum('nlcd,ldf->nlcf', column_piece, up_part, preferred_element_typ...  15.1 us
    all_gather x1, blocking collectives, per_device(): column_piece = lax.all_gather(arrived, 'tp', axis=3, tiled=True)  14.1 us
    all_to_all x1, waiting for transfers between devices, per_device(): lax.all_to_all(expert_output, 'ae', split_axis=0, concat_axis=0, tiled=True)  9.48 us
    all_gather x1, blocking collectives, per_device(): full_state = lax.all_gather(hidden_state, 'tp', axis=1, tiled=True)  5.66 us
    all_to_all x1, starting transfers between devices, per_device(): lax.all_to_all(outgoing, 'ae', split_axis=0, concat_axis=0, tiled=True)  5.43 us
  transfers between devices with their start and end apart: 3, of which 2 were waited for; matrix products, arithmetic and copies ran while one was open for 34% of the time, Pallas kernels for 0%

commit v1 on v0

v1 whole, which is shorter than its diff:
```python
import functools
import math

import jax
import jax.numpy as jnp
from jax import lax
from jax.experimental import pallas as pl
from jax.experimental.pallas import tpu as pltpu
from jax.sharding import PartitionSpec as P

EPSILON = 1e-05
LANES = 128
MIB = 2**20
NT = (((1,), (1,)), ((), ()))
TN = (((0,), (0,)), ((), ()))
VMEM = pltpu.VMEM


def in_vmem(count):
    return [pl.BlockSpec(memory_space=VMEM)] * count


def in_hbm(count):
    return [pl.BlockSpec(memory_space=pl.ANY)] * count


def column_of(row, size):
    wide = jnp.broadcast_to(row, (size, size))
    at = lax.broadcasted_iota(jnp.int32, (size, size), 0)
    own = at == lax.broadcasted_iota(jnp.int32, (size, size), 1)
    return jnp.sum(jnp.where(own, wide, 0.0), axis=1, keepdims=True)


def attention_kernel(
    ahead, tokens, queries, new_kv, lengths, routes, kv, w_up, payload, *rest
):
    if ahead:
        early, cached, sems, early_sem = rest
        fetch = pltpu.make_async_copy(w_up.at[pl.ds(0, ahead)], early, early_sem)
    else:
        cached, sems = rest
    loads = [pltpu.make_async_copy(kv.at[i], cached.at[i], sems.at[i]) for i in range(2)]
    for load in loads:
        load.start()
    if ahead:
        fetch.start()
    row_count, slice_width = tokens.shape
    local_heads, context, head_width = cached.shape[2:]
    per_key = slice_width // (local_heads * head_width)
    scale = 1.0 / math.sqrt(head_width)
    span = row_count * context

    picks = jnp.zeros((row_count, LANES), jnp.float32)
    lane = lax.broadcasted_iota(jnp.int32, (row_count, LANES), 1).astype(jnp.float32)
    for k in range(routes.shape[0]):
        chosen = column_of(routes[k : k + 1, :].astype(jnp.float32), row_count)
        picks = jnp.where(lane == chosen, 1.0, picks)
    payload[:, slice_width:] = picks.astype(jnp.bfloat16)

    limit = column_of(lengths[...].astype(jnp.float32), row_count)
    row = lax.broadcasted_iota(jnp.int32, (row_count, 1), 0).astype(jnp.float32)
    first = row * context
    last = first + limit
    first = jnp.concatenate([first] * per_key, axis=0)
    last = jnp.concatenate([last] * per_key, axis=0)
    place = lax.broadcasted_iota(jnp.int32, (per_key * row_count, span), 1).astype(jnp.float32)
    visible = (place >= first) & (place < last)

    def head_columns(ref, head):
        return ref[:, head * head_width : (head + 1) * head_width]

    loads[0].wait()
    probs, own_probs = [], []
    for g in range(local_heads):
        heads = jnp.concatenate(
            [head_columns(queries, g * per_key + i) for i in range(per_key)], axis=0
        )
        keys = cached[0, :, g].reshape(span, head_width)
        scores = lax.dot_general(heads, keys, NT, preferred_element_type=jnp.float32) * scale
        fresh = new_kv[0, :, g * head_width : (g + 1) * head_width].astype(jnp.float32)
        fresh = jnp.concatenate([fresh] * per_key, axis=0)
        own = jnp.sum(heads.astype(jnp.float32) * fresh, axis=1, keepdims=True) * scale
        weights = jnp.where(visible, jnp.exp(scores), 0.0)
        own = jnp.exp(own)
        total = jnp.sum(weights, axis=1, keepdims=True) + own
        probs.append((weights / total).astype(jnp.bfloat16))
        own_probs.append((own / total).astype(jnp.bfloat16).astype(jnp.float32))
    loads[1].wait()
    for g in range(local_heads):
        values = cached[1, :, g].reshape(span, head_width)
        mixed = jnp.dot(probs[g], values, preferred_element_type=jnp.float32)
        fresh = new_kv[1, :, g * head_width : (g + 1) * head_width].astype(jnp.float32)
        for i in range(per_key):
            part = slice(i * row_count, (i + 1) * row_count)
            head = g * per_key + i
            attended = mixed[part] + own_probs[g][part] * fresh
            state = head_columns(tokens, head).astype(jnp.float32) + attended
            payload[:, head * head_width : (head + 1) * head_width] = state.astype(jnp.bfloat16)
    if ahead:
        fetch.wait()


def attend(ahead, tokens, queries, kv, new_kv, lengths, routes, w_up):
    row_count, slice_width = tokens.shape
    payload = jax.ShapeDtypeStruct((row_count, slice_width + LANES), jnp.bfloat16)
    outs = [payload]
    scratch = [VMEM(kv.shape, kv.dtype), pltpu.SemaphoreType.DMA((2,))]
    if ahead:
        outs.append(VMEM((ahead,) + w_up.shape[1:], w_up.dtype))
        scratch.append(pltpu.SemaphoreType.DMA)
    return pl.pallas_call(
        functools.partial(attention_kernel, ahead),
        out_shape=outs,
        in_specs=in_vmem(5) + in_hbm(2),
        out_specs=in_vmem(len(outs)),
        scratch_shapes=scratch,
        compiler_params=pltpu.CompilerParams(vmem_limit_bytes=16 * MIB),
        name="attention",
    )(tokens, queries, new_kv, lengths[None, :], routes.T, kv, w_up)


def stage_kernel(start, count, w_up, payload, held, sem):
    del payload
    copy = pltpu.make_async_copy(w_up.at[pl.ds(start, count)], held, sem)
    copy.start()
    copy.wait()


def stage(start, count, w_up, payload):
    nbytes = 2 * count * w_up.shape[1] * w_up.shape[2]
    return pl.pallas_call(
        functools.partial(stage_kernel, start, count),
        out_shape=VMEM((count,) + w_up.shape[1:], w_up.dtype),
        in_specs=in_hbm(2),
        out_specs=pl.BlockSpec(memory_space=VMEM),
        scratch_shapes=[pltpu.SemaphoreType.DMA],
        compiler_params=pltpu.CompilerParams(vmem_limit_bytes=MIB),
        cost_estimate=pl.CostEstimate(flops=0, bytes_accessed=2 * nbytes, transcendentals=0),
        name="stage",
    )(w_up, payload)


def chunk_width(width):
    return next(c for c in (512, 384, 256, 128) if width % c == 0)


def expert_kernel(plan, n_early, n_out, placement, router, w_up, w_down, *refs):
    pieces, places, halves, relative, n_slots = plan
    piece_refs, refs = refs[:pieces], refs[pieces:]
    early_refs, refs = refs[:n_early], refs[n_early:]
    out_refs, refs = refs[:n_out], refs[n_out:]
    state, hidden, late, ring, late_sem, ring_sems = refs
    rows, width = state.shape
    slice_width = width // halves
    local_experts, units, _ = w_up.shape
    experts = router.shape[0]
    ae = lax.axis_index("ae")
    tp = lax.axis_index("tp") if relative else 0

    def half_start(half):
        return pl.multiple_of((tp ^ half if relative else half) * slice_width, LANES)

    n_late = late.shape[0]
    fetch = pltpu.make_async_copy(w_up.at[pl.ds(local_experts - n_late, n_late)], late, late_sem)
    fetch.start()
    step = ring.shape[2]
    per_half = slice_width // step
    chunks = halves * per_half

    def load(i):
        half = halves - 1 - i // per_half
        start = pl.multiple_of(half_start(half) + (i % per_half) * step, LANES)
        slot = i % n_slots
        return pltpu.make_async_copy(
            w_down.at[:, pl.ds(start, step)], ring.at[slot], ring_sems.at[slot]
        )

    for i in range(min(n_slots, chunks)):
        load(i).start()

    picks = [None] * (rows // 16)
    for ref, spots in zip(piece_refs, places):
        for index, block, half in spots:
            value = ref[...] if index is None else ref[index]
            state[block * 16 : (block + 1) * 16, pl.ds(half_start(half), slice_width)] = value[
                :, :slice_width
            ]
            picks[block] = value[:, slice_width:]
    picked = jnp.concatenate(picks, axis=0).astype(jnp.float32).T[:experts]
    squares = jnp.zeros((rows, LANES), jnp.float32)
    for i in range(width // LANES):
        part = state[:, i * LANES : (i + 1) * LANES].astype(jnp.float32)
        squares = squares + part * part
    square_sum = jnp.sum(squares.T, axis=0, keepdims=True)
    inverse = lax.rsqrt(square_sum / width + EPSILON)
    logits = lax.dot_general(router[...], state[...], NT, preferred_element_type=jnp.float32)
    gates = jnp.where(picked > 0.0, jnp.exp(logits * inverse), 0.0)
    gates = gates / jnp.sum(gates, axis=0, keepdims=True)

    parts = []
    for ref in early_refs:
        parts += [(ref, i) for i in range(ref.shape[0])]
    parts += [(late, i) for i in range(n_late)]
    for p, (ref, i) in enumerate(parts):
        if ref is late and i == 0:
            fetch.wait()
        gate = jnp.zeros((1, rows), jnp.float32)
        for e in range(experts):
            gate = jnp.where(placement[e] == ae * local_experts + p, gates[e : e + 1], gate)
        up = lax.dot_general(ref[i], state[...], NT, preferred_element_type=jnp.float32)
        up = up * inverse
        act = up / (1.0 + jnp.exp(-up)) * gate
        hidden[p * units : (p + 1) * units, :] = act.astype(jnp.bfloat16)

    shares = rows // n_out
    for i in range(chunks):
        load(i).wait()
        half, at = halves - 1 - i // per_half, (i % per_half) * step
        total = lax.dot_general(
            hidden[...], ring[i % n_slots], TN, preferred_element_type=jnp.float32
        )
        if i + n_slots < chunks:
            load(i + n_slots).start()
        for n, out in enumerate(out_refs):
            out[half, :, at : at + step] = total[n * shares : (n + 1) * shares].astype(out.dtype)


def run_experts(plan, out_types, placement, router, w_up, w_down, pieces, early, rows):
    halves = plan[2]
    local_experts, units, width = w_up.shape
    n_late = local_experts - sum(e.shape[0] for e in early)
    step = chunk_width(width // halves)
    n_out = len(out_types)
    scratch = [
        VMEM((rows, width), jnp.bfloat16),
        VMEM((local_experts * units, rows), jnp.bfloat16),
        VMEM((n_late, units, width), jnp.bfloat16),
        VMEM((plan[4], local_experts * units, step), jnp.bfloat16),
        pltpu.SemaphoreType.DMA,
        pltpu.SemaphoreType.DMA((plan[4],)),
    ]
    return pl.pallas_call(
        functools.partial(expert_kernel, plan, len(early), n_out),
        out_shape=[
            jax.ShapeDtypeStruct((halves, rows // n_out, width // halves), t) for t in out_types
        ],
        in_specs=[pl.BlockSpec(memory_space=pltpu.SMEM)]
        + in_vmem(1)
        + in_hbm(2)
        + in_vmem(len(pieces) + len(early)),
        out_specs=in_vmem(n_out),
        scratch_shapes=scratch,
        compiler_params=pltpu.CompilerParams(vmem_limit_bytes=37 * MIB),
        name="experts",
    )(
        placement,
        router,
        w_up,
        w_down,
        *pieces,
        *[pltpu.with_memory_space_constraint(e, VMEM) for e in early],
    )


def pair_kernel(mine, other, kept, *sent):
    halves, rows, _ = mine.shape
    for i in range(rows // 16):
        for half in range(halves):
            part = slice(i * 16, (i + 1) * 16)
            total = mine[half, part, :] + other[half, part, :].astype(jnp.float32)
            at = i * halves + half
            if at == 0:
                kept[...] = total
            else:
                sent[at - 1][...] = total.astype(jnp.bfloat16)


def pair_sum(mine, other):
    halves, rows, width = mine.shape
    blocks = halves * rows // 16
    outs = [jax.ShapeDtypeStruct((16, width), jnp.float32)]
    outs += [jax.ShapeDtypeStruct((16, width), jnp.bfloat16)] * (blocks - 1)
    return pl.pallas_call(
        pair_kernel,
        out_shape=outs,
        in_specs=in_vmem(2),
        out_specs=in_vmem(blocks),
        compiler_params=pltpu.CompilerParams(vmem_limit_bytes=8 * MIB),
        name="core_sum",
    )(mine, other)


def sum_kernel(kept, *refs):
    total = kept[...]
    for ref in refs[:-1]:
        total = total + ref[...].astype(jnp.float32)
    refs[-1][...] = total.astype(jnp.bfloat16)


def chip_sum(kept, received):
    return pl.pallas_call(
        sum_kernel,
        out_shape=jax.ShapeDtypeStruct(kept.shape, jnp.bfloat16),
        in_specs=in_vmem(1 + len(received)),
        out_specs=pl.BlockSpec(memory_space=VMEM),
        compiler_params=pltpu.CompilerParams(vmem_limit_bytes=4 * MIB),
        name="chip_sum",
    )(kept, *received)


def per_device(
    tokens, queries, kv_cache, new_kv, lengths, routes, placement, router_weight, w_up, w_down
):
    n_ae, n_tp, n_sub = lax.axis_size("ae"), lax.axis_size("tp"), lax.axis_size("sub")
    row_count, slice_width = tokens.shape
    local_experts, units, model_width = w_down.shape
    w_up = jnp.swapaxes(w_up, 1, 2)
    w_down = w_down.reshape(local_experts * units, model_width)
    router = router_weight.T
    rows = n_ae * n_sub * row_count

    ahead, behind = local_experts // 4, local_experts // 2
    payload, *early = attend(ahead, tokens, queries, kv_cache, new_kv, lengths, routes, w_up)

    direct = n_tp == 2 and n_sub == 2 and n_ae in (2, 4) and row_count == 16
    if not direct:
        pieces = [lax.all_gather(payload, ("ae", "sub", "tp"), axis=0)]
        blocks = n_ae * n_sub
        places = [[(b * n_tp + t, b, t) for b in range(blocks) for t in range(n_tp)]]
        plan = (1, places, n_tp, False, 2)
        if behind:
            early.append(stage(ahead, behind, w_up, payload))
        (total,) = run_experts(
            plan, [jnp.float32], placement, router, w_up, w_down, pieces, early, rows
        )
        total = total.reshape(n_tp, blocks, row_count, slice_width).swapaxes(0, 1)
        total = lax.psum_scatter(
            total.reshape(blocks * n_tp, row_count, slice_width),
            ("ae", "sub", "tp"),
            scatter_dimension=0,
            tiled=True,
        )
        return total.reshape(row_count, slice_width).astype(jnp.bfloat16)

    def swap(value, da, dt, ds):
        pairs = [
            (
                (a * n_tp + t) * n_sub + s,
                ((a ^ da) * n_tp + (t ^ dt)) * n_sub + (s ^ ds),
            )
            for a in range(n_ae)
            for t in range(n_tp)
            for s in range(n_sub)
        ]
        return lax.ppermute(value, ("ae", "tp", "sub"), pairs)

    partners = [(da, dt) for da in range(n_ae) for dt in range(n_tp)]
    near = [payload] + [swap(payload, da, dt, 0) for da, dt in partners[1:]]
    pieces = near + [swap(piece, 0, 0, 1) for piece in near]
    places = [[(None, ds * n_ae + da, dt)] for ds in range(n_sub) for da, dt in partners]
    if behind:
        early.append(stage(ahead, behind, w_up, payload))
    plan = (len(pieces), places, n_tp, True, 4)
    mine, other = run_experts(
        plan, [jnp.float32, jnp.bfloat16], placement, router, w_up, w_down, pieces, early, rows
    )
    kept, *sent = pair_sum(mine, swap(other, 0, 0, 1))
    received = [swap(part, da, dt, 0) for part, (da, dt) in zip(sent, partners[1:])]
    return chip_sum(kept, received)


def solution(mesh):
    placed = (
        P(("grp", "ae", "sub"), "tp"),
        P(("grp", "ae", "sub"), "tp"),
        P(None, ("grp", "ae", "sub"), "tp", None, None),
        P(None, ("grp", "ae", "sub"), "tp"),
        P(("grp", "ae", "sub")),
        P(("grp", "ae", "sub"), None),
        P(),
        P(),
        P("ae", None, ("tp", "sub")),
        P("ae", ("tp", "sub"), None),
    )
    return jax.shard_map(
        per_device,
        mesh=mesh,
        in_specs=placed,
        out_specs=P(("grp", "ae", "sub"), "tp"),
        check_vma=False,
    )
```

time: 216 us -> 90.3 us (0.42)
  local copies, waits for them, and re-layouts: 80.7 us -> 17.5 us
  matrix products: 40.2 us -> 0 us
  Pallas kernels: 0 us -> 35.3 us
  waiting for transfers between devices: 41.4 us -> 11.5 us
  blocking collectives: 21.9 us -> 0 us
  starting transfers between devices: 10 us -> 25.3 us
  between operations: 13.5 us -> 0.24 us
  other arithmetic: 5.99 us -> 0 us
    reshape x8 -> x0, local copies, waits for them, and re-layouts: 75.9 us -> none  [the longest x1 71.8 us: per_device(): down_part.reshape(local_experts, down_part.shape[1], heads_axis, slice_wi...]
    dot_general x7 -> x0, matrix products: 40.2 us -> none  [the longest x1 20.9 us: per_device(): jnp.einsum('nlcf,lftd->tnlcd', expert_hidden, shaped_down, preferred_elem...]
    pallas_call x0 -> x5, Pallas kernels: none -> 35.3 us  [the longest x1 30 us: run_experts(): pl.pallas_call(functools.partial(expert_kernel, plan, len(early), n_out),...]
    reduce_scatter x1 -> x0, waiting for transfers between devices: 31.9 us -> none  [per_device(): lax.psum_scatter(term, ('tp', 'sub'), scatter_dimension=0, tiled=True)]
    ppermute x0 -> x23, starting transfers between devices: none -> 25.3 us  [swap(): return lax.ppermute(value, ('ae', 'tp', 'sub'), pairs)]
    all_gather x3 -> x0, blocking collectives: 21.9 us -> none  [the longest x1 14.1 us: per_device(): column_piece = lax.all_gather(arrived, 'tp', axis=3, tiled=True)]
    unnamed x5 -> x48, local copies, waits for them, and re-layouts: 0.77 us -> 17.5 us
    ppermute x0 -> x23, waiting for transfers between devices: none -> 11.5 us  [swap(): return lax.ppermute(value, ('ae', 'tp', 'sub'), pairs)]
  transfers between devices with their start and end apart: 3 -> 23, of which waited for: 2 -> 8; matrix products, arithmetic and copies ran while one was open for 34% -> 0% of each run, Pallas kernels for 0% -> 1%
where the time goes in v1:
time: 90.3 us; the launch traced here: 89.8 us
  Pallas kernels  35.3 us (39%)
  starting transfers between devices  25.3 us (28%)
  local copies, waits for them, and re-layouts  17.5 us (19%)
  waiting for transfers between devices  11.5 us (13%)
    pallas_call x1, Pallas kernels, run_experts(): pl.pallas_call(functools.partial(expert_kernel, plan, len(early), n_out),...  30 us
    ppermute x23, starting transfers between devices, swap(): return lax.ppermute(value, ('ae', 'tp', 'sub'), pairs)  25.3 us
    unnamed x48, local copies, waits for them, and re-layouts  17.5 us
    ppermute x23, waiting for transfers between devices, swap(): return lax.ppermute(value, ('ae', 'tp', 'sub'), pairs)  11.5 us
    pallas_call x1, Pallas kernels, attend(): pl.pallas_call(functools.partial(attention_kernel, ahead), out_shape=outs...  3.51 us
  transfers between devices with their start and end apart: 23, of which 8 were waited for; matrix products, arithmetic and copies ran while one was open for 0% of the time, Pallas kernels for 1%

profile of v1, /device:TPU:0, one launch (start us, length us, event | category | flops | bytes accessed | tf_op | source)
XLA Modules:
  0.0 89.8 jit_solution(10887810755558429949)
XLA Ops:
  0.0 1.6 %copy-done.1 = bf16[2,16,4,64,128]{4,3,2,1,0:T(8,128)(2,1)S(1)} copy-done((bf16[2,16,4,64,128]{4,3,2,1,0:T(8,128)(2,1)S(1)}, bf16[2,16,4,64,128]{4,3,2,1,0:T(8,128)(2,1)}, u32[]{:S(2)}) %copy-start.1) | copy-done | bytes 2097176
  1.6 0.8 copy-done.4
  2.4 0.8 copy-done.5
  3.2 0.8 copy-done.6
  5.3 3.5 %attention.1 = (bf16[16,1664]{1,0:T(8,128)(2,1)S(1)}, bf16[1,1344,3072]{2,1,0:T(8,128)(2,1)S(1)}) custom-call(bf16[16,1536]{1,0:T(8,128)(2,1)S(1)} %copy-done.4, bf16[16,1536]{1,0:T(8,128)(2,1)S(1)} %copy-done.5, bf16[2,16,512]{2,1,0:T(8,128)(2,1)S(1)} %copy-done.6, s32[1,16]{1,0:T(1,128)S(1)} %bitcast.9, s32[4,16]{1,0:T(4,128)S(1)} %bitcast.8, ...), custom_call_target="tpu_custom_call" | custom-call | tf_op jit(solution)/shard_map/attention/pallas_call | solution.py:111
  9.3 5.6 %collective-permute-start.6 = (bf16[16,1664]{1,0:T(8,128)(2,1)S(1)}, bf16[16,1664]{1,0:T(8,128)(2,1)S(1)}, u32[]{:S(2)}, u32[]{:S(2)}) collective-permute-start(bf16[16,1664]{1,0:T(8,128)(2,1)S(1)} %get-tuple-element.17.payload.refs_0_), channel_id=1, source_target_pairs={{0,14},{1,15},{2,12},{3,13},{4,10},{5,11},{6,8},{7,9},{8,6},{9,7},... | collective-permute-start | bytes 159752 | tf_op jit(solution)/shard_map/ppermute | solution.py:355
  15.2 0.8 collective-permute-start.4
  15.9 2.0 %collective-permute-start.3 = (bf16[16,1664]{1,0:T(8,128)(2,1)S(1)}, bf16[16,1664]{1,0:T(8,128)(2,1)S(1)}, u32[]{:S(2)}, u32[]{:S(2)}) collective-permute-start(bf16[16,1664]{1,0:T(8,128)(2,1)S(1)} %get-tuple-element.17.payload.refs_0_), channel_id=1, source_target_pairs={{0,8},{1,9},{2,10},{3,11},{4,12},{5,13},{6,14},{7,15},{8,0},{9,1},... | collective-permute-start | bytes 159752 | tf_op jit(solution)/shard_map/ppermute | solution.py:355
  17.9 2.4 %collective-permute-start.2 = (bf16[16,1664]{1,0:T(8,128)(2,1)S(1)}, bf16[16,1664]{1,0:T(8,128)(2,1)S(1)}, u32[]{:S(2)}, u32[]{:S(2)}) collective-permute-start(bf16[16,1664]{1,0:T(8,128)(2,1)S(1)} %get-tuple-element.17.payload.refs_0_), channel_id=1, source_target_pairs={{0,6},{1,7},{2,4},{3,5},{4,2},{5,3},{6,0},{7,1},{8,14},{9,15},{10,... | collective-permute-start | bytes 159752 | tf_op jit(solution)/shard_map/ppermute | solution.py:355
  21.9 1.7 %collective-permute-done.4.refs_5_ = bf16[16,1664]{1,0:T(8,128)(2,1)S(1)} collective-permute-done((bf16[16,1664]{1,0:T(8,128)(2,1)S(1)}, bf16[16,1664]{1,0:T(8,128)(2,1)S(1)}, u32[]{:S(2)}, u32[]{:S(2)}) %collective-permute-start.4) | collective-permute-done | bytes 53280 | tf_op jit(solution)/shard_map/ppermute | solution.py:355
  23.7 1.0 %collective-permute-done.3.refs_4_ = bf16[16,1664]{1,0:T(8,128)(2,1)S(1)} collective-permute-done((bf16[16,1664]{1,0:T(8,128)(2,1)S(1)}, bf16[16,1664]{1,0:T(8,128)(2,1)S(1)}, u32[]{:S(2)}, u32[]{:S(2)}) %collective-permute-start.3) | collective-permute-done | bytes 53280 | tf_op jit(solution)/shard_map/ppermute | solution.py:355
  26.5 10.4 %copy-done = bf16[4,3072,1344]{1,2,0:T(8,128)(2,1)S(1)} copy-done((bf16[4,3072,1344]{1,2,0:T(8,128)(2,1)S(1)}, bf16[4,3072,1344]{1,2,0:T(8,128)(2,1)}, u32[]{:S(2)}) %copy-start) | copy-done | bytes 33030168
  36.9 1.1 %stage.1.refs_17_ = bf16[2,1344,3072]{2,1,0:T(8,128)(2,1)S(1)} custom-call(bf16[4,1344,3072]{2,1,0:T(8,128)(2,1)S(1)} %bitcast.7, bf16[16,1664]{1,0:T(8,128)(2,1)S(1)} %get-tuple-element.17.payload.refs_0_), custom_call_target="tpu_custom_call" | custom-call | bytes 33030144 | tf_op jit(solution)/shard_map/stage/pallas_call | solution.py:131
  38.8 30.0 %experts.1 = (f32[2,64,1536]{2,1,0:T(8,128)}, bf16[2,64,1536]{2,1,0:T(8,128)(2,1)}) custom-call(s32[16]{0:T(128)} %placement.1, bf16[16,3072]{1,0:T(8,128)(2,1)} %bitcast.11, bf16[4,1344,3072]{2,1,0:T(8,128)(2,1)} %bitcast.6, bf16[5376,3072]{1,0:T(8,128)(2,1)} %bitcast.10, bf16[16,1664]{1,0:T(8,128)(2,1)} %copy-done.3, bf16[16,1664]{1,0:T(8,128)(2,1)} %copy-done.16, ...), custom_call_target="tpu_custom_call" | custom-call | tf_op jit(solution)/shard_map/experts/pallas_call | solution.py:242
  69.1 1.7 %collective-permute-done.15.other = bf16[2,64,1536]{2,1,0:T(8,128)(2,1)S(1)} collective-permute-done((bf16[2,64,1536]{2,1,0:T(8,128)(2,1)}, bf16[2,64,1536]{2,1,0:T(8,128)(2,1)S(1)}, u32[]{:S(2)}, u32[]{:S(2)}) %collective-permute-start.15) | collective-permute-done | bytes 393248 | tf_op jit(solution)/shard_map/ppermute | solution.py:355
  70.8 1.1 %copy-done.2 = f32[2,64,1536]{2,1,0:T(8,128)S(1)} copy-done((f32[2,64,1536]{2,1,0:T(8,128)S(1)}, f32[2,64,1536]{2,1,0:T(8,128)}, u32[]{:S(2)}) %copy-start.2) | copy-done | bytes 786456
  72.0 1.1 %collective-permute-start.16 = (bf16[16,1536]{1,0:T(8,128)(2,1)S(1)}, bf16[16,1536]{1,0:T(8,128)(2,1)S(1)}, u32[]{:S(2)}, u32[]{:S(2)}) collective-permute-start(bf16[16,1536]{1,0:T(8,128)(2,1)S(1)} %get-tuple-element.22), channel_id=1, source_target_pairs={{0,2},{1,3},{2,0},{3,1},{4,6},{5,7},{6,4},{7,5},{8,10},{9,11},{10,... | collective-permute-start | bytes 147464 | tf_op jit(solution)/shard_map/ppermute | solution.py:355
  73.5 2.1 %collective-permute-start.18 = (bf16[16,1536]{1,0:T(8,128)(2,1)S(1)}, bf16[16,1536]{1,0:T(8,128)(2,1)S(1)}, u32[]{:S(2)}, u32[]{:S(2)}) collective-permute-start(bf16[16,1536]{1,0:T(8,128)(2,1)S(1)} %get-tuple-element.24), channel_id=1, source_target_pairs={{0,6},{1,7},{2,4},{3,5},{4,2},{5,3},{6,0},{7,1},{8,14},{9,15},{10,... | collective-permute-start | bytes 147464 | tf_op jit(solution)/shard_map/ppermute | solution.py:355
  75.6 2.4 %collective-permute-start.19 = (bf16[16,1536]{1,0:T(8,128)(2,1)S(1)}, bf16[16,1536]{1,0:T(8,128)(2,1)S(1)}, u32[]{:S(2)}, u32[]{:S(2)}) collective-permute-start(bf16[16,1536]{1,0:T(8,128)(2,1)S(1)} %get-tuple-element.25), channel_id=1, source_target_pairs={{0,8},{1,9},{2,10},{3,11},{4,12},{5,13},{6,14},{7,15},{8,0},{9,1},... | collective-permute-start | bytes 147464 | tf_op jit(solution)/shard_map/ppermute | solution.py:355
  77.9 1.1 %collective-permute-start.20 = (bf16[16,1536]{1,0:T(8,128)(2,1)S(1)}, bf16[16,1536]{1,0:T(8,128)(2,1)S(1)}, u32[]{:S(2)}, u32[]{:S(2)}) collective-permute-start(bf16[16,1536]{1,0:T(8,128)(2,1)S(1)} %get-tuple-element.26), channel_id=1, source_target_pairs={{0,10},{1,11},{2,8},{3,9},{4,14},{5,15},{6,12},{7,13},{8,2},{9,3},... | collective-permute-start | bytes 147464 | tf_op jit(solution)/shard_map/ppermute | solution.py:355
  79.0 3.4 %collective-permute-start.21 = (bf16[16,1536]{1,0:T(8,128)(2,1)S(1)}, bf16[16,1536]{1,0:T(8,128)(2,1)S(1)}, u32[]{:S(2)}, u32[]{:S(2)}) collective-permute-start(bf16[16,1536]{1,0:T(8,128)(2,1)S(1)} %get-tuple-element.27), channel_id=1, source_target_pairs={{0,12},{1,13},{2,14},{3,15},{4,8},{5,9},{6,10},{7,11},{8,4},{9,5},... | collective-permute-start | bytes 147464 | tf_op jit(solution)/shard_map/ppermute | solution.py:355
  82.3 0.9 collective-permute-start.22
  83.2 2.7 %collective-permute-done.20.refs_4_ = bf16[16,1536]{1,0:T(8,128)(2,1)S(1)} collective-permute-done((bf16[16,1536]{1,0:T(8,128)(2,1)S(1)}, bf16[16,1536]{1,0:T(8,128)(2,1)S(1)}, u32[]{:S(2)}, u32[]{:S(2)}) %collective-permute-start.20) | collective-permute-done | bytes 49184 | tf_op jit(solution)/shard_map/ppermute | solution.py:355
  85.9 3.2 %collective-permute-done.22.refs_6_ = bf16[16,1536]{1,0:T(8,128)(2,1)S(1)} collective-permute-done((bf16[16,1536]{1,0:T(8,128)(2,1)S(1)}, bf16[16,1536]{1,0:T(8,128)(2,1)S(1)}, u32[]{:S(2)}, u32[]{:S(2)}) %collective-permute-start.22) | collective-permute-done | bytes 49184 | tf_op jit(solution)/shard_map/ppermute | solution.py:355
  (75 shorter events, 7.7 us)
Async XLA Ops:
  8.8 29.2 %copy-start.3 = (bf16[16,1664]{1,0:T(8,128)(2,1)}, bf16[16,1664]{1,0:T(8,128)(2,1)S(1)}, u32[]{:S(2)}) copy-start(bf16[16,1664]{1,0:T(8,128)(2,1)S(1)} %get-tuple-element.17.payload.refs_0_) | copy-start | bytes 159748
  8.8 9.1 %collective-permute-start.7 = (bf16[16,1664]{1,0:T(8,128)(2,1)S(1)}, bf16[16,1664]{1,0:T(8,128)(2,1)S(1)}, u32[]{:S(2)}, u32[]{:S(2)}) collective-permute-start(bf16[16,1664]{1,0:T(8,128)(2,1)S(1)} %get-tuple-element.17.payload.refs_0_), channel_id=1, source_target_pairs={{0,1},{1,0},{2,3},{3,2},{4,5},{5,4},{6,7},{7,6},{8,9},{9,8},{10,11... | collective-permute-start | bytes 159752 | tf_op jit(solution)/shard_map/ppermute | solution.py:355
  9.3 11.0 %collective-permute-start.6 = (bf16[16,1664]{1,0:T(8,128)(2,1)S(1)}, bf16[16,1664]{1,0:T(8,128)(2,1)S(1)}, u32[]{:S(2)}, u32[]{:S(2)}) collective-permute-start(bf16[16,1664]{1,0:T(8,128)(2,1)S(1)} %get-tuple-element.17.payload.refs_0_), channel_id=1, source_target_pairs={{0,14},{1,15},{2,12},{3,13},{4,10},{5,11},{6,8},{7,9},{8,6},{9,7},... | collective-permute-start | bytes 159752 | tf_op jit(solution)/shard_map/ppermute | solution.py:355
  14.9 6.5 %collective-permute-start.5 = (bf16[16,1664]{1,0:T(8,128)(2,1)S(1)}, bf16[16,1664]{1,0:T(8,128)(2,1)S(1)}, u32[]{:S(2)}, u32[]{:S(2)}) collective-permute-start(bf16[16,1664]{1,0:T(8,128)(2,1)S(1)} %get-tuple-element.17.payload.refs_0_), channel_id=1, source_target_pairs={{0,12},{1,13},{2,14},{3,15},{4,8},{5,9},{6,10},{7,11},{8,4},{9,5},... | collective-permute-start | bytes 159752 | tf_op jit(solution)/shard_map/ppermute | solution.py:355
  15.2 8.5 %collective-permute-start.4 = (bf16[16,1664]{1,0:T(8,128)(2,1)S(1)}, bf16[16,1664]{1,0:T(8,128)(2,1)S(1)}, u32[]{:S(2)}, u32[]{:S(2)}) collective-permute-start(bf16[16,1664]{1,0:T(8,128)(2,1)S(1)} %get-tuple-element.17.payload.refs_0_), channel_id=1, source_target_pairs={{0,10},{1,11},{2,8},{3,9},{4,14},{5,15},{6,12},{7,13},{8,2},{9,3},... | collective-permute-start | bytes 159752 | tf_op jit(solution)/shard_map/ppermute | solution.py:355
  15.9 8.7 %collective-permute-start.3 = (bf16[16,1664]{1,0:T(8,128)(2,1)S(1)}, bf16[16,1664]{1,0:T(8,128)(2,1)S(1)}, u32[]{:S(2)}, u32[]{:S(2)}) collective-permute-start(bf16[16,1664]{1,0:T(8,128)(2,1)S(1)} %get-tuple-element.17.payload.refs_0_), channel_id=1, source_target_pairs={{0,8},{1,9},{2,10},{3,11},{4,12},{5,13},{6,14},{7,15},{8,0},{9,1},... | collective-permute-start | bytes 159752 | tf_op jit(solution)/shard_map/ppermute | solution.py:355
  17.9 7.2 %collective-permute-start.2 = (bf16[16,1664]{1,0:T(8,128)(2,1)S(1)}, bf16[16,1664]{1,0:T(8,128)(2,1)S(1)}, u32[]{:S(2)}, u32[]{:S(2)}) collective-permute-start(bf16[16,1664]{1,0:T(8,128)(2,1)S(1)} %get-tuple-element.17.payload.refs_0_), channel_id=1, source_target_pairs={{0,6},{1,7},{2,4},{3,5},{4,2},{5,3},{6,0},{7,1},{8,14},{9,15},{10,... | collective-permute-start | bytes 159752 | tf_op jit(solution)/shard_map/ppermute | solution.py:355
  20.3 5.1 %collective-permute-start.1 = (bf16[16,1664]{1,0:T(8,128)(2,1)S(1)}, bf16[16,1664]{1,0:T(8,128)(2,1)S(1)}, u32[]{:S(2)}, u32[]{:S(2)}) collective-permute-start(bf16[16,1664]{1,0:T(8,128)(2,1)S(1)} %get-tuple-element.17.payload.refs_0_), channel_id=1, source_target_pairs={{0,4},{1,5},{2,6},{3,7},{4,0},{5,1},{6,2},{7,3},{8,12},{9,13},{10,... | collective-permute-start | bytes 159752 | tf_op jit(solution)/shard_map/ppermute | solution.py:355
  21.4 4.3 %collective-permute-start = (bf16[16,1664]{1,0:T(8,128)(2,1)S(1)}, bf16[16,1664]{1,0:T(8,128)(2,1)S(1)}, u32[]{:S(2)}, u32[]{:S(2)}) collective-permute-start(bf16[16,1664]{1,0:T(8,128)(2,1)S(1)} %get-tuple-element.17.payload.refs_0_), channel_id=1, source_target_pairs={{0,2},{1,3},{2,0},{3,1},{4,6},{5,7},{6,4},{7,5},{8,10},{9,11},{10,... | collective-permute-start | bytes 159752 | tf_op jit(solution)/shard_map/ppermute | solution.py:355
  23.7 2.3 %collective-permute-start.14 = (bf16[16,1664]{1,0:T(8,128)(2,1)S(1)}, bf16[16,1664]{1,0:T(8,128)(2,1)S(1)}, u32[]{:S(2)}, u32[]{:S(2)}) collective-permute-start(bf16[16,1664]{1,0:T(8,128)(2,1)S(1)} %collective-permute-done.6.refs_7_), channel_id=1, source_target_pairs={{0,1},{1,0},{2,3},{3,2},{4,5},{5,4},{6,7},{7,6},{8,9},{9,8},{10,11... | collective-permute-start | bytes 159752 | tf_op jit(solution)/shard_map/ppermute | solution.py:355
  24.6 1.6 %collective-permute-start.13 = (bf16[16,1664]{1,0:T(8,128)(2,1)S(1)}, bf16[16,1664]{1,0:T(8,128)(2,1)S(1)}, u32[]{:S(2)}, u32[]{:S(2)}) collective-permute-start(bf16[16,1664]{1,0:T(8,128)(2,1)S(1)} %collective-permute-done.5.refs_6_), channel_id=1, source_target_pairs={{0,1},{1,0},{2,3},{3,2},{4,5},{5,4},{6,7},{7,6},{8,9},{9,8},{10,11... | collective-permute-start | bytes 159752 | tf_op jit(solution)/shard_map/ppermute | solution.py:355
  25.2 12.9 %collective-permute-start.12 = (bf16[16,1664]{1,0:T(8,128)(2,1)S(1)}, bf16[16,1664]{1,0:T(8,128)(2,1)S(1)}, u32[]{:S(2)}, u32[]{:S(2)}) collective-permute-start(bf16[16,1664]{1,0:T(8,128)(2,1)S(1)} %collective-permute-done.4.refs_5_), channel_id=1, source_target_pairs={{0,1},{1,0},{2,3},{3,2},{4,5},{5,4},{6,7},{7,6},{8,9},{9,8},{10,11... | collective-permute-start | bytes 159752 | tf_op jit(solution)/shard_map/ppermute | solution.py:355
  25.4 12.7 %collective-permute-start.11 = (bf16[16,1664]{1,0:T(8,128)(2,1)S(1)}, bf16[16,1664]{1,0:T(8,128)(2,1)S(1)}, u32[]{:S(2)}, u32[]{:S(2)}) collective-permute-start(bf16[16,1664]{1,0:T(8,128)(2,1)S(1)} %collective-permute-done.3.refs_4_), channel_id=1, source_target_pairs={{0,1},{1,0},{2,3},{3,2},{4,5},{5,4},{6,7},{7,6},{8,9},{9,8},{10,11... | collective-permute-start | bytes 159752 | tf_op jit(solution)/shard_map/ppermute | solution.py:355
  25.7 12.4 %collective-permute-start.10 = (bf16[16,1664]{1,0:T(8,128)(2,1)S(1)}, bf16[16,1664]{1,0:T(8,128)(2,1)S(1)}, u32[]{:S(2)}, u32[]{:S(2)}) collective-permute-start(bf16[16,1664]{1,0:T(8,128)(2,1)S(1)} %collective-permute-done.2.refs_3_), channel_id=1, source_target_pairs={{0,1},{1,0},{2,3},{3,2},{4,5},{5,4},{6,7},{7,6},{8,9},{9,8},{10,11... | collective-permute-start | bytes 159752 | tf_op jit(solution)/shard_map/ppermute | solution.py:355
  26.0 12.2 %collective-permute-start.9 = (bf16[16,1664]{1,0:T(8,128)(2,1)S(1)}, bf16[16,1664]{1,0:T(8,128)(2,1)S(1)}, u32[]{:S(2)}, u32[]{:S(2)}) collective-permute-start(bf16[16,1664]{1,0:T(8,128)(2,1)S(1)} %collective-permute-done.1.refs_2_), channel_id=1, source_target_pairs={{0,1},{1,0},{2,3},{3,2},{4,5},{5,4},{6,7},{7,6},{8,9},{9,8},{10,11... | collective-permute-start | bytes 159752 | tf_op jit(solution)/shard_map/ppermute | solution.py:355
  26.2 12.0 %collective-permute-start.8 = (bf16[16,1664]{1,0:T(8,128)(2,1)S(1)}, bf16[16,1664]{1,0:T(8,128)(2,1)S(1)}, u32[]{:S(2)}, u32[]{:S(2)}) collective-permute-start(bf16[16,1664]{1,0:T(8,128)(2,1)S(1)} %collective-permute-done.refs_1_), channel_id=1, source_target_pairs={{0,1},{1,0},{2,3},{3,2},{4,5},{5,4},{6,7},{7,6},{8,9},{9,8},{10,11... | collective-permute-start | bytes 159752 | tf_op jit(solution)/shard_map/ppermute | solution.py:355
  68.8 2.0 %collective-permute-start.15 = (bf16[2,64,1536]{2,1,0:T(8,128)(2,1)}, bf16[2,64,1536]{2,1,0:T(8,128)(2,1)S(1)}, u32[]{:S(2)}, u32[]{:S(2)}) collective-permute-start(bf16[2,64,1536]{2,1,0:T(8,128)(2,1)} %get-tuple-element.20), channel_id=1, source_target_pairs={{0,1},{1,0},{2,3},{3,2},{4,5},{5,4},{6,7},{7,6},{8,9},{9,8},{10,11... | collective-permute-start | bytes 1179656 | tf_op jit(solution)/shard_map/ppermute | solution.py:355
  72.0 7.0 %collective-permute-start.16 = (bf16[16,1536]{1,0:T(8,128)(2,1)S(1)}, bf16[16,1536]{1,0:T(8,128)(2,1)S(1)}, u32[]{:S(2)}, u32[]{:S(2)}) collective-permute-start(bf16[16,1536]{1,0:T(8,128)(2,1)S(1)} %get-tuple-element.22), channel_id=1, source_target_pairs={{0,2},{1,3},{2,0},{3,1},{4,6},{5,7},{6,4},{7,5},{8,10},{9,11},{10,... | collective-permute-start | bytes 147464 | tf_op jit(solution)/shard_map/ppermute | solution.py:355
  73.1 9.2 %collective-permute-start.17 = (bf16[16,1536]{1,0:T(8,128)(2,1)S(1)}, bf16[16,1536]{1,0:T(8,128)(2,1)S(1)}, u32[]{:S(2)}, u32[]{:S(2)}) collective-permute-start(bf16[16,1536]{1,0:T(8,128)(2,1)S(1)} %get-tuple-element.23), channel_id=1, source_target_pairs={{0,4},{1,5},{2,6},{3,7},{4,0},{5,1},{6,2},{7,3},{8,12},{9,13},{10,... | collective-permute-start | bytes 147464 | tf_op jit(solution)/shard_map/ppermute | solution.py:355
  73.5 9.7 %collective-permute-start.18 = (bf16[16,1536]{1,0:T(8,128)(2,1)S(1)}, bf16[16,1536]{1,0:T(8,128)(2,1)S(1)}, u32[]{:S(2)}, u32[]{:S(2)}) collective-permute-start(bf16[16,1536]{1,0:T(8,128)(2,1)S(1)} %get-tuple-element.24), channel_id=1, source_target_pairs={{0,6},{1,7},{2,4},{3,5},{4,2},{5,3},{6,0},{7,1},{8,14},{9,15},{10,... | collective-permute-start | bytes 147464 | tf_op jit(solution)/shard_map/ppermute | solution.py:355
  75.6 7.7 %collective-permute-start.19 = (bf16[16,1536]{1,0:T(8,128)(2,1)S(1)}, bf16[16,1536]{1,0:T(8,128)(2,1)S(1)}, u32[]{:S(2)}, u32[]{:S(2)}) collective-permute-start(bf16[16,1536]{1,0:T(8,128)(2,1)S(1)} %get-tuple-element.25), channel_id=1, source_target_pairs={{0,8},{1,9},{2,10},{3,11},{4,12},{5,13},{6,14},{7,15},{8,0},{9,1},... | collective-permute-start | bytes 147464 | tf_op jit(solution)/shard_map/ppermute | solution.py:355
  77.9 8.0 %collective-permute-start.20 = (bf16[16,1536]{1,0:T(8,128)(2,1)S(1)}, bf16[16,1536]{1,0:T(8,128)(2,1)S(1)}, u32[]{:S(2)}, u32[]{:S(2)}) collective-permute-start(bf16[16,1536]{1,0:T(8,128)(2,1)S(1)} %get-tuple-element.26), channel_id=1, source_target_pairs={{0,10},{1,11},{2,8},{3,9},{4,14},{5,15},{6,12},{7,13},{8,2},{9,3},... | collective-permute-start | bytes 147464 | tf_op jit(solution)/shard_map/ppermute | solution.py:355
  79.0 6.9 %collective-permute-start.21 = (bf16[16,1536]{1,0:T(8,128)(2,1)S(1)}, bf16[16,1536]{1,0:T(8,128)(2,1)S(1)}, u32[]{:S(2)}, u32[]{:S(2)}) collective-permute-start(bf16[16,1536]{1,0:T(8,128)(2,1)S(1)} %get-tuple-element.27), channel_id=1, source_target_pairs={{0,12},{1,13},{2,14},{3,15},{4,8},{5,9},{6,10},{7,11},{8,4},{9,5},... | collective-permute-start | bytes 147464 | tf_op jit(solution)/shard_map/ppermute | solution.py:355
  82.3 6.8 %collective-permute-start.22 = (bf16[16,1536]{1,0:T(8,128)(2,1)S(1)}, bf16[16,1536]{1,0:T(8,128)(2,1)S(1)}, u32[]{:S(2)}, u32[]{:S(2)}) collective-permute-start(bf16[16,1536]{1,0:T(8,128)(2,1)S(1)} %get-tuple-element.28), channel_id=1, source_target_pairs={{0,14},{1,15},{2,12},{3,13},{4,10},{5,11},{6,8},{7,9},{8,6},{9,7},... | collective-permute-start | bytes 147464 | tf_op jit(solution)/shard_map/ppermute | solution.py:355
  (23 other events, 164.0 us)

commit v2 on v1

--- a/solution.py
+++ b/solution.py
@@ -21,7 +21,7 @@
 
 
 def in_hbm(count):
-    return [pl.BlockSpec(memory_space=pl.ANY)] * count
+    return [pl.BlockSpec(memory_space=pltpu.HBM)] * count
 
 
 def column_of(row, size):
@@ -31,25 +31,36 @@
     return jnp.sum(jnp.where(own, wide, 0.0), axis=1, keepdims=True)
 
 
-def attention_kernel(
-    ahead, tokens, queries, new_kv, lengths, routes, kv, w_up, payload, *rest
-):
-    if ahead:
-        early, cached, sems, early_sem = rest
-        fetch = pltpu.make_async_copy(w_up.at[pl.ds(0, ahead)], early, early_sem)
-    else:
-        cached, sems = rest
-    loads = [pltpu.make_async_copy(kv.at[i], cached.at[i], sems.at[i]) for i in range(2)]
-    for load in loads:
-        load.start()
-    if ahead:
-        fetch.start()
+def attention_kernel(n_early, *refs):
+    sources, refs = refs[:7], refs[7:]
+    outs, refs = refs[: 1 + (n_early > 0)], refs[1 + (n_early > 0) :]
+    payload = outs[0]
+    lengths, routes, tokens, queries, new_kv, cached, sems = refs
+    moves = [
+        (sources[0].at[0], cached.at[0]),
+        (sources[1], queries),
+        (sources[2], new_kv),
+        (sources[5], routes),
+        (sources[4], lengths),
+        (sources[0].at[1], cached.at[1]),
+        (sources[3], tokens),
+    ]
+    if n_early:
+        moves.append((sources[6].at[pl.ds(0, n_early)], outs[1]))
+    copies = [
+        pltpu.make_async_copy(source, target, sems.at[i])
+        for i, (source, target) in enumerate(moves)
+    ]
+    for copy in copies:
+        copy.start()
     row_count, slice_width = tokens.shape
     local_heads, context, head_width = cached.shape[2:]
     per_key = slice_width // (local_heads * head_width)
     scale = 1.0 / math.sqrt(head_width)
     span = row_count * context
 
+    for copy in copies[:5]:
+        copy.wait()
     picks = jnp.zeros((row_count, LANES), jnp.float32)
     lane = lax.broadcasted_iota(jnp.int32, (row_count, LANES), 1).astype(jnp.float32)
     for k in range(routes.shape[0]):
@@ -69,7 +80,6 @@
     def head_columns(ref, head):
         return ref[:, head * head_width : (head + 1) * head_width]
 
-    loads[0].wait()
     probs, own_probs = [], []
     for g in range(local_heads):
         heads = jnp.concatenate(
@@ -85,7 +95,8 @@
         total = jnp.sum(weights, axis=1, keepdims=True) + own
         probs.append((weights / total).astype(jnp.bfloat16))
         own_probs.append((own / total).astype(jnp.bfloat16).astype(jnp.float32))
-    loads[1].wait()
+    for copy in copies[5:7]:
+        copy.wait()
     for g in range(local_heads):
         values = cached[1, :, g].reshape(span, head_width)
         mixed = jnp.dot(probs[g], values, preferred_element_type=jnp.float32)
@@ -96,48 +107,31 @@
             attended = mixed[part] + own_probs[g][part] * fresh
             state = head_columns(tokens, head).astype(jnp.float32) + attended
             payload[:, head * head_width : (head + 1) * head_width] = state.astype(jnp.bfloat16)
-    if ahead:
-        fetch.wait()
-
-
-def attend(ahead, tokens, queries, kv, new_kv, lengths, routes, w_up):
+    for copy in copies[7:]:
+        copy.wait()
+
+
+def attend(n_early, tokens, queries, kv, new_kv, lengths, routes, w_up):
     row_count, slice_width = tokens.shape
-    payload = jax.ShapeDtypeStruct((row_count, slice_width + LANES), jnp.bfloat16)
-    outs = [payload]
-    scratch = [VMEM(kv.shape, kv.dtype), pltpu.SemaphoreType.DMA((2,))]
-    if ahead:
-        outs.append(VMEM((ahead,) + w_up.shape[1:], w_up.dtype))
-        scratch.append(pltpu.SemaphoreType.DMA)
+    lengths, routes = lengths[None, :], routes.T
+    big = (kv, queries, new_kv, tokens, lengths, routes, w_up)
+    held = (lengths, routes, tokens, queries, new_kv, kv)
+    outs = [VMEM((row_count, slice_width + LANES), jnp.bfloat16)]
+    if n_early:
+        outs.append(VMEM((n_early, w_up.shape[1]), w_up.dtype))
     return pl.pallas_call(
-        functools.partial(attention_kernel, ahead),
+        functools.partial(attention_kernel, n_early),
         out_shape=outs,
-        in_specs=in_vmem(5) + in_hbm(2),
+        in_specs=in_hbm(len(big)),
         out_specs=in_vmem(len(outs)),
-        scratch_shapes=scratch,
+        scratch_shapes=[VMEM(a.shape, a.dtype) for a in held] + [pltpu.SemaphoreType.DMA((8,))],
         compiler_params=pltpu.CompilerParams(vmem_limit_bytes=16 * MIB),
         name="attention",
-    )(tokens, queries, new_kv, lengths[None, :], routes.T, kv, w_up)
-
-
-def stage_kernel(start, count, w_up, payload, held, sem):
-    del payload
-    copy = pltpu.make_async_copy(w_up.at[pl.ds(start, count)], held, sem)
-    copy.start()
-    copy.wait()
-
-
-def stage(start, count, w_up, payload):
-    nbytes = 2 * count * w_up.shape[1] * w_up.shape[2]
-    return pl.pallas_call(
-        functools.partial(stage_kernel, start, count),
-        out_shape=VMEM((count,) + w_up.shape[1:], w_up.dtype),
-        in_specs=in_hbm(2),
-        out_specs=pl.BlockSpec(memory_space=VMEM),
-        scratch_shapes=[pltpu.SemaphoreType.DMA],
-        compiler_params=pltpu.CompilerParams(vmem_limit_bytes=MIB),
-        cost_estimate=pl.CostEstimate(flops=0, bytes_accessed=2 * nbytes, transcendentals=0),
-        name="stage",
-    )(w_up, payload)
+    )(*[from_hbm(a) for a in big])
+
+
+def from_hbm(value):
+    return pltpu.with_memory_space_constraint(value, pltpu.HBM)
 
 
 def chunk_width(width):
@@ -147,22 +141,31 @@
 def expert_kernel(plan, n_early, n_out, placement, router, w_up, w_down, *refs):
     pieces, places, halves, relative, n_slots = plan
     piece_refs, refs = refs[:pieces], refs[pieces:]
-    early_refs, refs = refs[:n_early], refs[n_early:]
+    early_refs, refs = refs[: n_early > 0], refs[n_early > 0 :]
     out_refs, refs = refs[:n_out], refs[n_out:]
-    state, hidden, late, ring, late_sem, ring_sems = refs
+    state, hidden, flat, late, ring, late_sems, ring_sems = refs
     rows, width = state.shape
     slice_width = width // halves
-    local_experts, units, _ = w_up.shape
+    total_units = w_up.shape[0]
     experts = router.shape[0]
+    local_experts = experts // lax.axis_size("ae")
+    units = total_units // local_experts
     ae = lax.axis_index("ae")
     tp = lax.axis_index("tp") if relative else 0
 
     def half_start(half):
         return pl.multiple_of((tp ^ half if relative else half) * slice_width, LANES)
 
-    n_late = late.shape[0]
-    fetch = pltpu.make_async_copy(w_up.at[pl.ds(local_experts - n_late, n_late)], late, late_sem)
-    fetch.start()
+    def fetch(i):
+        return pltpu.make_async_copy(
+            w_up.at[pl.ds(n_early + i * units, units)],
+            late.at[pl.ds(i * units, units)],
+            late_sems.at[i],
+        )
+
+    n_late = late.shape[0] // units
+    for i in range(n_late):
+        fetch(i).start()
     step = ring.shape[2]
     per_half = slice_width // step
     chunks = halves * per_half
@@ -197,66 +200,76 @@
     gates = jnp.where(picked > 0.0, jnp.exp(logits * inverse), 0.0)
     gates = gates / jnp.sum(gates, axis=0, keepdims=True)
 
-    parts = []
-    for ref in early_refs:
-        parts += [(ref, i) for i in range(ref.shape[0])]
-    parts += [(late, i) for i in range(n_late)]
-    for p, (ref, i) in enumerate(parts):
-        if ref is late and i == 0:
-            fetch.wait()
+    span = up_span(units)
+    for p in range(local_experts):
         gate = jnp.zeros((1, rows), jnp.float32)
         for e in range(experts):
             gate = jnp.where(placement[e] == ae * local_experts + p, gates[e : e + 1], gate)
-        up = lax.dot_general(ref[i], state[...], NT, preferred_element_type=jnp.float32)
-        up = up * inverse
-        act = up / (1.0 + jnp.exp(-up)) * gate
-        hidden[p * units : (p + 1) * units, :] = act.astype(jnp.bfloat16)
+        if p * units < n_early:
+            weights, base = early_refs[0], p * units
+        else:
+            weights, base = late, p * units - n_early
+            fetch(base // units).wait()
+        for start in range(0, units, span):
+            up = lax.dot_general(
+                weights[base + start : base + start + span],
+                state[...],
+                NT,
+                preferred_element_type=jnp.float32,
+            )
+            up = up * inverse
+            act = up / (1.0 + jnp.exp(-up)) * gate
+            at = p * units + start
+            hidden[at : at + span, :] = act.astype(jnp.bfloat16)
+    flat[...] = hidden[...].T
 
     shares = rows // n_out
     for i in range(chunks):
         load(i).wait()
         half, at = halves - 1 - i // per_half, (i % per_half) * step
-        total = lax.dot_general(
-            hidden[...], ring[i % n_slots], TN, preferred_element_type=jnp.float32
-        )
+        total = jnp.dot(flat[...], ring[i % n_slots], preferred_element_type=jnp.float32)
         if i + n_slots < chunks:
             load(i + n_slots).start()
         for n, out in enumerate(out_refs):
             out[half, :, at : at + step] = total[n * shares : (n + 1) * shares].astype(out.dtype)
 
 
-def run_experts(plan, out_types, placement, router, w_up, w_down, pieces, early, rows):
+def up_span(units):
+    return 336 if units % 336 == 0 else units
+
+
+def run_experts(plan, n_early, out_types, placement, router, w_up, w_down, pieces, early, rows):
     halves = plan[2]
-    local_experts, units, width = w_up.shape
-    n_late = local_experts - sum(e.shape[0] for e in early)
+    total_units, width = w_up.shape
+    local_experts = router.shape[0] // lax.axis_size("ae")
+    units = total_units // local_experts
     step = chunk_width(width // halves)
     n_out = len(out_types)
     scratch = [
         VMEM((rows, width), jnp.bfloat16),
-        VMEM((local_experts * units, rows), jnp.bfloat16),
-        VMEM((n_late, units, width), jnp.bfloat16),
-        VMEM((plan[4], local_experts * units, step), jnp.bfloat16),
-        pltpu.SemaphoreType.DMA,
+        VMEM((total_units, rows), jnp.bfloat16),
+        VMEM((rows, total_units), jnp.bfloat16),
+        VMEM((total_units - n_early, width), jnp.bfloat16),
+        VMEM((plan[4], total_units, step), jnp.bfloat16),
+        pltpu.SemaphoreType.DMA(((total_units - n_early) // units,)),
         pltpu.SemaphoreType.DMA((plan[4],)),
     ]
     return pl.pallas_call(
-        functools.partial(expert_kernel, plan, len(early), n_out),
-        out_shape=[
-            jax.ShapeDtypeStruct((halves, rows // n_out, width // halves), t) for t in out_types
-        ],
+        functools.partial(expert_kernel, plan, n_early, n_out),
+        out_shape=[VMEM((halves, rows // n_out, width // halves), t) for t in out_types],
         in_specs=[pl.BlockSpec(memory_space=pltpu.SMEM)]
         + in_vmem(1)
         + in_hbm(2)
         + in_vmem(len(pieces) + len(early)),
         out_specs=in_vmem(n_out),
         scratch_shapes=scratch,
-        compiler_params=pltpu.CompilerParams(vmem_limit_bytes=37 * MIB),
+        compiler_params=pltpu.CompilerParams(vmem_limit_bytes=50 * MIB),
         name="experts",
     )(
         placement,
         router,
-        w_up,
-        w_down,
+        from_hbm(w_up),
+        from_hbm(w_down),
         *pieces,
         *[pltpu.with_memory_space_constraint(e, VMEM) for e in early],
     )
@@ -314,13 +327,15 @@
     n_ae, n_tp, n_sub = lax.axis_size("ae"), lax.axis_size("tp"), lax.axis_size("sub")
     row_count, slice_width = tokens.shape
     local_experts, units, model_width = w_down.shape
-    w_up = jnp.swapaxes(w_up, 1, 2)
+    w_up = jnp.swapaxes(w_up, 1, 2).reshape(local_experts * units, model_width)
     w_down = w_down.reshape(local_experts * units, model_width)
     router = router_weight.T
     rows = n_ae * n_sub * row_count
 
-    ahead, behind = local_experts // 4, local_experts // 2
-    payload, *early = attend(ahead, tokens, queries, kv_cache, new_kv, lengths, routes, w_up)
+    n_early = local_experts // 4 * units
+    payload, *early = attend(
+        n_early, tokens, queries, kv_cache, new_kv, lengths, routes, w_up
+    )
 
     direct = n_tp == 2 and n_sub == 2 and n_ae in (2, 4) and row_count == 16
     if not direct:
@@ -328,10 +343,8 @@
         blocks = n_ae * n_sub
         places = [[(b * n_tp + t, b, t) for b in range(blocks) for t in range(n_tp)]]
         plan = (1, places, n_tp, False, 2)
-        if behind:
-            early.append(stage(ahead, behind, w_up, payload))
         (total,) = run_experts(
-            plan, [jnp.float32], placement, router, w_up, w_down, pieces, early, rows
+            plan, n_early, [jnp.float32], placement, router, w_up, w_down, pieces, early, rows
         )
         total = total.reshape(n_tp, blocks, row_count, slice_width).swapaxes(0, 1)
         total = lax.psum_scatter(
@@ -358,11 +371,10 @@
     near = [payload] + [swap(payload, da, dt, 0) for da, dt in partners[1:]]
     pieces = near + [swap(piece, 0, 0, 1) for piece in near]
     places = [[(None, ds * n_ae + da, dt)] for ds in range(n_sub) for da, dt in partners]
-    if behind:
-        early.append(stage(ahead, behind, w_up, payload))
     plan = (len(pieces), places, n_tp, True, 4)
+    types = [jnp.float32, jnp.bfloat16]
     mine, other = run_experts(
-        plan, [jnp.float32, jnp.bfloat16], placement, router, w_up, w_down, pieces, early, rows
+        plan, n_early, types, placement, router, w_up, w_down, pieces, early, rows
     )
     kept, *sent = pair_sum(mine, swap(other, 0, 0, 1))
     received = [swap(part, da, dt, 0) for part, (da, dt) in zip(sent, partners[1:])]

time: 90.3 us -> 66.9 us (0.74)
  local copies, waits for them, and re-layouts: 17.5 us -> 0.56 us
  Pallas kernels: 35.3 us -> 28.4 us
    unnamed x48 -> x32, local copies, waits for them, and re-layouts: 17.5 us -> 0.56 us
    pallas_call x3 -> x2, Pallas kernels: 34.6 us -> 27.7 us  [the longest x1 23.6 us: run_experts(): pl.pallas_call(functools.partial(expert_kernel, plan, n_early, n_out), ou...]
  transfers between devices with their start and end apart: 23 -> 23, of which waited for: 8 -> 12; matrix products, arithmetic and copies ran while one was open for 0% -> 0% of each run, Pallas kernels for 1% -> 0%
where the time goes in v2:
time: 66.9 us; the launch traced here: 66.8 us
  Pallas kernels  28.4 us (42%)
  starting transfers between devices  25.3 us (38%)
  waiting for transfers between devices  12.3 us (18%)
    ppermute x23, starting transfers between devices, swap(): return lax.ppermute(value, ('ae', 'tp', 'sub'), pairs)  25.3 us
    pallas_call x1, Pallas kernels, run_experts(): pl.pallas_call(functools.partial(expert_kernel, plan, n_early, n_out), ou...  23.6 us
    ppermute x23, waiting for transfers between devices, swap(): return lax.ppermute(value, ('ae', 'tp', 'sub'), pairs)  12.3 us
    pallas_call x1, Pallas kernels, attend(): pl.pallas_call(functools.partial(attention_kernel, n_early), out_shape=ou...  4.15 us
  transfers between devices with their start and end apart: 23, of which 12 were waited for; matrix products, arithmetic and copies ran while one was open for 0% of the time, Pallas kernels for 0%

profile of v2, /device:TPU:0, one launch (start us, length us, event | category | flops | bytes accessed | tf_op | source)
XLA Modules:
  0.0 66.8 jit_solution(2502697282901387348)
XLA Ops:
  0.0 4.1 %attention.1 = (bf16[16,1664]{1,0:T(8,128)(2,1)S(1)}, bf16[1344,3072]{1,0:T(8,128)(2,1)S(1)}) custom-call(bf16[2,16,4,64,128]{4,3,2,1,0:T(8,128)(2,1)} %refs_0_.1, bf16[16,1536]{1,0:T(8,128)(2,1)} %refs_1_.1, bf16[2,16,512]{2,1,0:T(8,128)(2,1)} %refs_2_.1, bf16[16,1536]{1,0:T(8,128)(2,1)} %refs_3_.1, s32[1,16]{1,0:T(1,128)} %bitcast.12, s32[4,16]{1,0:T(4,128)} %bitcast.11, ...), custom_call_target="tpu_custom_call" | custom-call | tf_op jit(solution)/shard_map/attention/pallas_call | solution.py:122
  4.2 0.5 collective-permute-start.7
  4.7 5.6 %collective-permute-start.6 = (bf16[16,1664]{1,0:T(8,128)(2,1)S(1)}, bf16[16,1664]{1,0:T(8,128)(2,1)S(1)}, u32[]{:S(2)}, u32[]{:S(2)}) collective-permute-start(bf16[16,1664]{1,0:T(8,128)(2,1)S(1)} %get-tuple-element.17.refs_0_), channel_id=1, source_target_pairs={{0,14},{1,15},{2,12},{3,13},{4,10},{5,11},{6,8},{7,9},{8,6},{9,7},... | collective-permute-start | bytes 159752 | tf_op jit(solution)/shard_map/ppermute | solution.py:368
  10.5 0.8 %collective-permute-start.4 = (bf16[16,1664]{1,0:T(8,128)(2,1)S(1)}, bf16[16,1664]{1,0:T(8,128)(2,1)S(1)}, u32[]{:S(2)}, u32[]{:S(2)}) collective-permute-start(bf16[16,1664]{1,0:T(8,128)(2,1)S(1)} %get-tuple-element.17.refs_0_), channel_id=1, source_target_pairs={{0,10},{1,11},{2,8},{3,9},{4,14},{5,15},{6,12},{7,13},{8,2},{9,3},... | collective-permute-start | bytes 159752 | tf_op jit(solution)/shard_map/ppermute | solution.py:368
  11.3 2.0 %collective-permute-start.3 = (bf16[16,1664]{1,0:T(8,128)(2,1)S(1)}, bf16[16,1664]{1,0:T(8,128)(2,1)S(1)}, u32[]{:S(2)}, u32[]{:S(2)}) collective-permute-start(bf16[16,1664]{1,0:T(8,128)(2,1)S(1)} %get-tuple-element.17.refs_0_), channel_id=1, source_target_pairs={{0,8},{1,9},{2,10},{3,11},{4,12},{5,13},{6,14},{7,15},{8,0},{9,1},... | collective-permute-start | bytes 159752 | tf_op jit(solution)/shard_map/ppermute | solution.py:368
  13.3 2.4 %collective-permute-start.2 = (bf16[16,1664]{1,0:T(8,128)(2,1)S(1)}, bf16[16,1664]{1,0:T(8,128)(2,1)S(1)}, u32[]{:S(2)}, u32[]{:S(2)}) collective-permute-start(bf16[16,1664]{1,0:T(8,128)(2,1)S(1)} %get-tuple-element.17.refs_0_), channel_id=1, source_target_pairs={{0,6},{1,7},{2,4},{3,5},{4,2},{5,3},{6,0},{7,1},{8,14},{9,15},{10,... | collective-permute-start | bytes 159752 | tf_op jit(solution)/shard_map/ppermute | solution.py:368
  15.7 0.7 %collective-permute-start.1 = (bf16[16,1664]{1,0:T(8,128)(2,1)S(1)}, bf16[16,1664]{1,0:T(8,128)(2,1)S(1)}, u32[]{:S(2)}, u32[]{:S(2)}) collective-permute-start(bf16[16,1664]{1,0:T(8,128)(2,1)S(1)} %get-tuple-element.17.refs_0_), channel_id=1, source_target_pairs={{0,4},{1,5},{2,6},{3,7},{4,0},{5,1},{6,2},{7,3},{8,12},{9,13},{10,... | collective-permute-start | bytes 159752 | tf_op jit(solution)/shard_map/ppermute | solution.py:368
  16.4 0.4 collective-permute-done.5.refs_6_
  16.8 0.5 collective-permute-start
  17.3 1.7 %collective-permute-done.4.refs_5_ = bf16[16,1664]{1,0:T(8,128)(2,1)S(1)} collective-permute-done((bf16[16,1664]{1,0:T(8,128)(2,1)S(1)}, bf16[16,1664]{1,0:T(8,128)(2,1)S(1)}, u32[]{:S(2)}, u32[]{:S(2)}) %collective-permute-start.4) | collective-permute-done | bytes 53280 | tf_op jit(solution)/shard_map/ppermute | solution.py:368
  19.0 1.0 %collective-permute-done.3.refs_4_ = bf16[16,1664]{1,0:T(8,128)(2,1)S(1)} collective-permute-done((bf16[16,1664]{1,0:T(8,128)(2,1)S(1)}, bf16[16,1664]{1,0:T(8,128)(2,1)S(1)}, u32[]{:S(2)}, u32[]{:S(2)}) %collective-permute-start.3) | collective-permute-done | bytes 53280 | tf_op jit(solution)/shard_map/ppermute | solution.py:368
  20.0 0.6 collective-permute-done.2.refs_3_
  23.4 23.6 %experts.1 = (f32[2,64,1536]{2,1,0:T(8,128)S(1)}, bf16[2,64,1536]{2,1,0:T(8,128)(2,1)S(1)}) custom-call(s32[16]{0:T(128)} %placement.1, bf16[16,3072]{1,0:T(8,128)(2,1)} %bitcast.10, bf16[5376,3072]{1,0:T(8,128)(2,1)} %bitcast.8, bf16[5376,3072]{1,0:T(8,128)(2,1)} %bitcast.9, bf16[16,1664]{1,0:T(8,128)(2,1)} %copy-done, bf16[16,1664]{1,0:T(8,128)(2,1)} %copy-done.8, ...), custom_call_target="tpu_custom_call" | custom-call | tf_op jit(solution)/shard_map/experts/pallas_call | solution.py:257
  47.0 0.3 collective-permute-start.15
  47.3 1.5 %collective-permute-done.15.other = bf16[2,64,1536]{2,1,0:T(8,128)(2,1)S(1)} collective-permute-done((bf16[2,64,1536]{2,1,0:T(8,128)(2,1)S(1)}, bf16[2,64,1536]{2,1,0:T(8,128)(2,1)S(1)}, u32[]{:S(2)}, u32[]{:S(2)}) %collective-permute-start.15) | collective-permute-done | bytes 393248 | tf_op jit(solution)/shard_map/ppermute | solution.py:368
  48.9 1.2 %collective-permute-start.16 = (bf16[16,1536]{1,0:T(8,128)(2,1)S(1)}, bf16[16,1536]{1,0:T(8,128)(2,1)S(1)}, u32[]{:S(2)}, u32[]{:S(2)}) collective-permute-start(bf16[16,1536]{1,0:T(8,128)(2,1)S(1)} %get-tuple-element.22), channel_id=1, source_target_pairs={{0,2},{1,3},{2,0},{3,1},{4,6},{5,7},{6,4},{7,5},{8,10},{9,11},{10,... | collective-permute-start | bytes 147464 | tf_op jit(solution)/shard_map/ppermute | solution.py:368
  50.2 2.2 %collective-permute-start.18 = (bf16[16,1536]{1,0:T(8,128)(2,1)S(1)}, bf16[16,1536]{1,0:T(8,128)(2,1)S(1)}, u32[]{:S(2)}, u32[]{:S(2)}) collective-permute-start(bf16[16,1536]{1,0:T(8,128)(2,1)S(1)} %get-tuple-element.24), channel_id=1, source_target_pairs={{0,6},{1,7},{2,4},{3,5},{4,2},{5,3},{6,0},{7,1},{8,14},{9,15},{10,... | collective-permute-start | bytes 147464 | tf_op jit(solution)/shard_map/ppermute | solution.py:368
  52.4 2.5 %collective-permute-start.19 = (bf16[16,1536]{1,0:T(8,128)(2,1)S(1)}, bf16[16,1536]{1,0:T(8,128)(2,1)S(1)}, u32[]{:S(2)}, u32[]{:S(2)}) collective-permute-start(bf16[16,1536]{1,0:T(8,128)(2,1)S(1)} %get-tuple-element.25), channel_id=1, source_target_pairs={{0,8},{1,9},{2,10},{3,11},{4,12},{5,13},{6,14},{7,15},{8,0},{9,1},... | collective-permute-start | bytes 147464 | tf_op jit(solution)/shard_map/ppermute | solution.py:368
  54.9 1.1 %collective-permute-start.20 = (bf16[16,1536]{1,0:T(8,128)(2,1)S(1)}, bf16[16,1536]{1,0:T(8,128)(2,1)S(1)}, u32[]{:S(2)}, u32[]{:S(2)}) collective-permute-start(bf16[16,1536]{1,0:T(8,128)(2,1)S(1)} %get-tuple-element.26), channel_id=1, source_target_pairs={{0,10},{1,11},{2,8},{3,9},{4,14},{5,15},{6,12},{7,13},{8,2},{9,3},... | collective-permute-start | bytes 147464 | tf_op jit(solution)/shard_map/ppermute | solution.py:368
  55.9 3.4 %collective-permute-start.21 = (bf16[16,1536]{1,0:T(8,128)(2,1)S(1)}, bf16[16,1536]{1,0:T(8,128)(2,1)S(1)}, u32[]{:S(2)}, u32[]{:S(2)}) collective-permute-start(bf16[16,1536]{1,0:T(8,128)(2,1)S(1)} %get-tuple-element.27), channel_id=1, source_target_pairs={{0,12},{1,13},{2,14},{3,15},{4,8},{5,9},{6,10},{7,11},{8,4},{9,5},... | collective-permute-start | bytes 147464 | tf_op jit(solution)/shard_map/ppermute | solution.py:368
  59.3 0.8 %collective-permute-start.22 = (bf16[16,1536]{1,0:T(8,128)(2,1)S(1)}, bf16[16,1536]{1,0:T(8,128)(2,1)S(1)}, u32[]{:S(2)}, u32[]{:S(2)}) collective-permute-start(bf16[16,1536]{1,0:T(8,128)(2,1)S(1)} %get-tuple-element.28), channel_id=1, source_target_pairs={{0,14},{1,15},{2,12},{3,13},{4,10},{5,11},{6,8},{7,9},{8,6},{9,7},... | collective-permute-start | bytes 147464 | tf_op jit(solution)/shard_map/ppermute | solution.py:368
  60.1 2.8 %collective-permute-done.20.refs_4_ = bf16[16,1536]{1,0:T(8,128)(2,1)S(1)} collective-permute-done((bf16[16,1536]{1,0:T(8,128)(2,1)S(1)}, bf16[16,1536]{1,0:T(8,128)(2,1)S(1)}, u32[]{:S(2)}, u32[]{:S(2)}) %collective-permute-start.20) | collective-permute-done | bytes 49184 | tf_op jit(solution)/shard_map/ppermute | solution.py:368
  62.9 3.2 %collective-permute-done.22.refs_6_ = bf16[16,1536]{1,0:T(8,128)(2,1)S(1)} collective-permute-done((bf16[16,1536]{1,0:T(8,128)(2,1)S(1)}, bf16[16,1536]{1,0:T(8,128)(2,1)S(1)}, u32[]{:S(2)}, u32[]{:S(2)}) %collective-permute-start.22) | collective-permute-done | bytes 49184 | tf_op jit(solution)/shard_map/ppermute | solution.py:368
  66.1 0.7 %chip_sum.1 = bf16[16,1536]{1,0:T(8,128)(2,1)} custom-call(f32[16,1536]{1,0:T(8,128)S(1)} %get-tuple-element.21.kept, bf16[16,1536]{1,0:T(8,128)(2,1)S(1)} %collective-permute-done.16.refs_0_, bf16[16,1536]{1,0:T(8,128)(2,1)S(1)} %collective-permute-done.17.refs_1_, bf16[16,1536]{1,0:T(8,128)(2,1)S(1)} %collective-permute-done.18.refs_2_, ...), custom_call_target="tpu_custom_call" | custom-call | tf_op jit(solution)/shard_map/chip_sum/pallas_call | solution.py:314
  (58 shorter events, 3.3 us)
Async XLA Ops:
  4.2 18.7 %copy-start = (bf16[16,1664]{1,0:T(8,128)(2,1)}, bf16[16,1664]{1,0:T(8,128)(2,1)S(1)}, u32[]{:S(2)}) copy-start(bf16[16,1664]{1,0:T(8,128)(2,1)S(1)} %get-tuple-element.17.refs_0_) | copy-start | bytes 159748
  4.2 9.1 %collective-permute-start.7 = (bf16[16,1664]{1,0:T(8,128)(2,1)S(1)}, bf16[16,1664]{1,0:T(8,128)(2,1)S(1)}, u32[]{:S(2)}, u32[]{:S(2)}) collective-permute-start(bf16[16,1664]{1,0:T(8,128)(2,1)S(1)} %get-tuple-element.17.refs_0_), channel_id=1, source_target_pairs={{0,1},{1,0},{2,3},{3,2},{4,5},{5,4},{6,7},{7,6},{8,9},{9,8},{10,11... | collective-permute-start | bytes 159752 | tf_op jit(solution)/shard_map/ppermute | solution.py:368
  4.7 11.0 %collective-permute-start.6 = (bf16[16,1664]{1,0:T(8,128)(2,1)S(1)}, bf16[16,1664]{1,0:T(8,128)(2,1)S(1)}, u32[]{:S(2)}, u32[]{:S(2)}) collective-permute-start(bf16[16,1664]{1,0:T(8,128)(2,1)S(1)} %get-tuple-element.17.refs_0_), channel_id=1, source_target_pairs={{0,14},{1,15},{2,12},{3,13},{4,10},{5,11},{6,8},{7,9},{8,6},{9,7},... | collective-permute-start | bytes 159752 | tf_op jit(solution)/shard_map/ppermute | solution.py:368
  10.3 6.5 %collective-permute-start.5 = (bf16[16,1664]{1,0:T(8,128)(2,1)S(1)}, bf16[16,1664]{1,0:T(8,128)(2,1)S(1)}, u32[]{:S(2)}, u32[]{:S(2)}) collective-permute-start(bf16[16,1664]{1,0:T(8,128)(2,1)S(1)} %get-tuple-element.17.refs_0_), channel_id=1, source_target_pairs={{0,12},{1,13},{2,14},{3,15},{4,8},{5,9},{6,10},{7,11},{8,4},{9,5},... | collective-permute-start | bytes 159752 | tf_op jit(solution)/shard_map/ppermute | solution.py:368
  10.5 8.5 %collective-permute-start.4 = (bf16[16,1664]{1,0:T(8,128)(2,1)S(1)}, bf16[16,1664]{1,0:T(8,128)(2,1)S(1)}, u32[]{:S(2)}, u32[]{:S(2)}) collective-permute-start(bf16[16,1664]{1,0:T(8,128)(2,1)S(1)} %get-tuple-element.17.refs_0_), channel_id=1, source_target_pairs={{0,10},{1,11},{2,8},{3,9},{4,14},{5,15},{6,12},{7,13},{8,2},{9,3},... | collective-permute-start | bytes 159752 | tf_op jit(solution)/shard_map/ppermute | solution.py:368
  11.3 8.7 %collective-permute-start.3 = (bf16[16,1664]{1,0:T(8,128)(2,1)S(1)}, bf16[16,1664]{1,0:T(8,128)(2,1)S(1)}, u32[]{:S(2)}, u32[]{:S(2)}) collective-permute-start(bf16[16,1664]{1,0:T(8,128)(2,1)S(1)} %get-tuple-element.17.refs_0_), channel_id=1, source_target_pairs={{0,8},{1,9},{2,10},{3,11},{4,12},{5,13},{6,14},{7,15},{8,0},{9,1},... | collective-permute-start | bytes 159752 | tf_op jit(solution)/shard_map/ppermute | solution.py:368
  13.3 7.2 %collective-permute-start.2 = (bf16[16,1664]{1,0:T(8,128)(2,1)S(1)}, bf16[16,1664]{1,0:T(8,128)(2,1)S(1)}, u32[]{:S(2)}, u32[]{:S(2)}) collective-permute-start(bf16[16,1664]{1,0:T(8,128)(2,1)S(1)} %get-tuple-element.17.refs_0_), channel_id=1, source_target_pairs={{0,6},{1,7},{2,4},{3,5},{4,2},{5,3},{6,0},{7,1},{8,14},{9,15},{10,... | collective-permute-start | bytes 159752 | tf_op jit(solution)/shard_map/ppermute | solution.py:368
  15.7 5.1 %collective-permute-start.1 = (bf16[16,1664]{1,0:T(8,128)(2,1)S(1)}, bf16[16,1664]{1,0:T(8,128)(2,1)S(1)}, u32[]{:S(2)}, u32[]{:S(2)}) collective-permute-start(bf16[16,1664]{1,0:T(8,128)(2,1)S(1)} %get-tuple-element.17.refs_0_), channel_id=1, source_target_pairs={{0,4},{1,5},{2,6},{3,7},{4,0},{5,1},{6,2},{7,3},{8,12},{9,13},{10,... | collective-permute-start | bytes 159752 | tf_op jit(solution)/shard_map/ppermute | solution.py:368
  16.8 4.3 %collective-permute-start = (bf16[16,1664]{1,0:T(8,128)(2,1)S(1)}, bf16[16,1664]{1,0:T(8,128)(2,1)S(1)}, u32[]{:S(2)}, u32[]{:S(2)}) collective-permute-start(bf16[16,1664]{1,0:T(8,128)(2,1)S(1)} %get-tuple-element.17.refs_0_), channel_id=1, source_target_pairs={{0,2},{1,3},{2,0},{3,1},{4,6},{5,7},{6,4},{7,5},{8,10},{9,11},{10,... | collective-permute-start | bytes 159752 | tf_op jit(solution)/shard_map/ppermute | solution.py:368
  19.0 2.3 %collective-permute-start.14 = (bf16[16,1664]{1,0:T(8,128)(2,1)S(1)}, bf16[16,1664]{1,0:T(8,128)(2,1)S(1)}, u32[]{:S(2)}, u32[]{:S(2)}) collective-permute-start(bf16[16,1664]{1,0:T(8,128)(2,1)S(1)} %collective-permute-done.6.refs_7_), channel_id=1, source_target_pairs={{0,1},{1,0},{2,3},{3,2},{4,5},{5,4},{6,7},{7,6},{8,9},{9,8},{10,11... | collective-permute-start | bytes 159752 | tf_op jit(solution)/shard_map/ppermute | solution.py:368
  20.0 1.6 %collective-permute-start.13 = (bf16[16,1664]{1,0:T(8,128)(2,1)S(1)}, bf16[16,1664]{1,0:T(8,128)(2,1)S(1)}, u32[]{:S(2)}, u32[]{:S(2)}) collective-permute-start(bf16[16,1664]{1,0:T(8,128)(2,1)S(1)} %collective-permute-done.5.refs_6_), channel_id=1, source_target_pairs={{0,1},{1,0},{2,3},{3,2},{4,5},{5,4},{6,7},{7,6},{8,9},{9,8},{10,11... | collective-permute-start | bytes 159752 | tf_op jit(solution)/shard_map/ppermute | solution.py:368
  20.5 1.3 %collective-permute-start.12 = (bf16[16,1664]{1,0:T(8,128)(2,1)S(1)}, bf16[16,1664]{1,0:T(8,128)(2,1)S(1)}, u32[]{:S(2)}, u32[]{:S(2)}) collective-permute-start(bf16[16,1664]{1,0:T(8,128)(2,1)S(1)} %collective-permute-done.4.refs_5_), channel_id=1, source_target_pairs={{0,1},{1,0},{2,3},{3,2},{4,5},{5,4},{6,7},{7,6},{8,9},{9,8},{10,11... | collective-permute-start | bytes 159752 | tf_op jit(solution)/shard_map/ppermute | solution.py:368
  20.8 1.2 %collective-permute-start.11 = (bf16[16,1664]{1,0:T(8,128)(2,1)S(1)}, bf16[16,1664]{1,0:T(8,128)(2,1)S(1)}, u32[]{:S(2)}, u32[]{:S(2)}) collective-permute-start(bf16[16,1664]{1,0:T(8,128)(2,1)S(1)} %collective-permute-done.3.refs_4_), channel_id=1, source_target_pairs={{0,1},{1,0},{2,3},{3,2},{4,5},{5,4},{6,7},{7,6},{8,9},{9,8},{10,11... | collective-permute-start | bytes 159752 | tf_op jit(solution)/shard_map/ppermute | solution.py:368
  21.0 1.2 %collective-permute-start.10 = (bf16[16,1664]{1,0:T(8,128)(2,1)S(1)}, bf16[16,1664]{1,0:T(8,128)(2,1)S(1)}, u32[]{:S(2)}, u32[]{:S(2)}) collective-permute-start(bf16[16,1664]{1,0:T(8,128)(2,1)S(1)} %collective-permute-done.2.refs_3_), channel_id=1, source_target_pairs={{0,1},{1,0},{2,3},{3,2},{4,5},{5,4},{6,7},{7,6},{8,9},{9,8},{10,11... | collective-permute-start | bytes 159752 | tf_op jit(solution)/shard_map/ppermute | solution.py:368
  21.3 1.2 %collective-permute-start.9 = (bf16[16,1664]{1,0:T(8,128)(2,1)S(1)}, bf16[16,1664]{1,0:T(8,128)(2,1)S(1)}, u32[]{:S(2)}, u32[]{:S(2)}) collective-permute-start(bf16[16,1664]{1,0:T(8,128)(2,1)S(1)} %collective-permute-done.1.refs_2_), channel_id=1, source_target_pairs={{0,1},{1,0},{2,3},{3,2},{4,5},{5,4},{6,7},{7,6},{8,9},{9,8},{10,11... | collective-permute-start | bytes 159752 | tf_op jit(solution)/shard_map/ppermute | solution.py:368
  21.6 1.2 %collective-permute-start.8 = (bf16[16,1664]{1,0:T(8,128)(2,1)S(1)}, bf16[16,1664]{1,0:T(8,128)(2,1)S(1)}, u32[]{:S(2)}, u32[]{:S(2)}) collective-permute-start(bf16[16,1664]{1,0:T(8,128)(2,1)S(1)} %collective-permute-done.refs_1_), channel_id=1, source_target_pairs={{0,1},{1,0},{2,3},{3,2},{4,5},{5,4},{6,7},{7,6},{8,9},{9,8},{10,11... | collective-permute-start | bytes 159752 | tf_op jit(solution)/shard_map/ppermute | solution.py:368
  47.0 1.8 %collective-permute-start.15 = (bf16[2,64,1536]{2,1,0:T(8,128)(2,1)S(1)}, bf16[2,64,1536]{2,1,0:T(8,128)(2,1)S(1)}, u32[]{:S(2)}, u32[]{:S(2)}) collective-permute-start(bf16[2,64,1536]{2,1,0:T(8,128)(2,1)S(1)} %get-tuple-element.20), channel_id=1, source_target_pairs={{0,1},{1,0},{2,3},{3,2},{4,5},{5,4},{6,7},{7,6},{8,9},{9,8},{10,11... | collective-permute-start | bytes 1179656 | tf_op jit(solution)/shard_map/ppermute | solution.py:368
  48.9 7.1 %collective-permute-start.16 = (bf16[16,1536]{1,0:T(8,128)(2,1)S(1)}, bf16[16,1536]{1,0:T(8,128)(2,1)S(1)}, u32[]{:S(2)}, u32[]{:S(2)}) collective-permute-start(bf16[16,1536]{1,0:T(8,128)(2,1)S(1)} %get-tuple-element.22), channel_id=1, source_target_pairs={{0,2},{1,3},{2,0},{3,1},{4,6},{5,7},{6,4},{7,5},{8,10},{9,11},{10,... | collective-permute-start | bytes 147464 | tf_op jit(solution)/shard_map/ppermute | solution.py:368
  50.1 9.2 %collective-permute-start.17 = (bf16[16,1536]{1,0:T(8,128)(2,1)S(1)}, bf16[16,1536]{1,0:T(8,128)(2,1)S(1)}, u32[]{:S(2)}, u32[]{:S(2)}) collective-permute-start(bf16[16,1536]{1,0:T(8,128)(2,1)S(1)} %get-tuple-element.23), channel_id=1, source_target_pairs={{0,4},{1,5},{2,6},{3,7},{4,0},{5,1},{6,2},{7,3},{8,12},{9,13},{10,... | collective-permute-start | bytes 147464 | tf_op jit(solution)/shard_map/ppermute | solution.py:368
  50.2 9.8 %collective-permute-start.18 = (bf16[16,1536]{1,0:T(8,128)(2,1)S(1)}, bf16[16,1536]{1,0:T(8,128)(2,1)S(1)}, u32[]{:S(2)}, u32[]{:S(2)}) collective-permute-start(bf16[16,1536]{1,0:T(8,128)(2,1)S(1)} %get-tuple-element.24), channel_id=1, source_target_pairs={{0,6},{1,7},{2,4},{3,5},{4,2},{5,3},{6,0},{7,1},{8,14},{9,15},{10,... | collective-permute-start | bytes 147464 | tf_op jit(solution)/shard_map/ppermute | solution.py:368
  52.4 7.7 %collective-permute-start.19 = (bf16[16,1536]{1,0:T(8,128)(2,1)S(1)}, bf16[16,1536]{1,0:T(8,128)(2,1)S(1)}, u32[]{:S(2)}, u32[]{:S(2)}) collective-permute-start(bf16[16,1536]{1,0:T(8,128)(2,1)S(1)} %get-tuple-element.25), channel_id=1, source_target_pairs={{0,8},{1,9},{2,10},{3,11},{4,12},{5,13},{6,14},{7,15},{8,0},{9,1},... | collective-permute-start | bytes 147464 | tf_op jit(solution)/shard_map/ppermute | solution.py:368
  54.9 8.0 %collective-permute-start.20 = (bf16[16,1536]{1,0:T(8,128)(2,1)S(1)}, bf16[16,1536]{1,0:T(8,128)(2,1)S(1)}, u32[]{:S(2)}, u32[]{:S(2)}) collective-permute-start(bf16[16,1536]{1,0:T(8,128)(2,1)S(1)} %get-tuple-element.26), channel_id=1, source_target_pairs={{0,10},{1,11},{2,8},{3,9},{4,14},{5,15},{6,12},{7,13},{8,2},{9,3},... | collective-permute-start | bytes 147464 | tf_op jit(solution)/shard_map/ppermute | solution.py:368
  55.9 7.0 %collective-permute-start.21 = (bf16[16,1536]{1,0:T(8,128)(2,1)S(1)}, bf16[16,1536]{1,0:T(8,128)(2,1)S(1)}, u32[]{:S(2)}, u32[]{:S(2)}) collective-permute-start(bf16[16,1536]{1,0:T(8,128)(2,1)S(1)} %get-tuple-element.27), channel_id=1, source_target_pairs={{0,12},{1,13},{2,14},{3,15},{4,8},{5,9},{6,10},{7,11},{8,4},{9,5},... | collective-permute-start | bytes 147464 | tf_op jit(solution)/shard_map/ppermute | solution.py:368
  59.3 6.8 %collective-permute-start.22 = (bf16[16,1536]{1,0:T(8,128)(2,1)S(1)}, bf16[16,1536]{1,0:T(8,128)(2,1)S(1)}, u32[]{:S(2)}, u32[]{:S(2)}) collective-permute-start(bf16[16,1536]{1,0:T(8,128)(2,1)S(1)} %get-tuple-element.28), channel_id=1, source_target_pairs={{0,14},{1,15},{2,12},{3,13},{4,10},{5,11},{6,8},{7,9},{8,6},{9,7},... | collective-permute-start | bytes 147464 | tf_op jit(solution)/shard_map/ppermute | solution.py:368
  (15 other events, 42.4 us)

commit v3 on v2

--- a/solution.py
+++ b/solution.py
@@ -134,16 +134,55 @@
     return pltpu.with_memory_space_constraint(value, pltpu.HBM)
 
 
+def stage_kernel(start, w_up, payload, held, sem):
+    del payload
+    copy = pltpu.make_async_copy(w_up.at[pl.ds(start, held.shape[0])], held, sem)
+    copy.start()
+    copy.wait()
+
+
+def stage(start, count, w_up, payload):
+    nbytes = 2 * count * w_up.shape[1]
+    return pl.pallas_call(
+        functools.partial(stage_kernel, start),
+        out_shape=VMEM((count, w_up.shape[1]), w_up.dtype),
+        in_specs=in_hbm(1) + in_vmem(1),
+        out_specs=pl.BlockSpec(memory_space=VMEM),
+        scratch_shapes=[pltpu.SemaphoreType.DMA],
+        compiler_params=pltpu.CompilerParams(vmem_limit_bytes=MIB),
+        cost_estimate=pl.CostEstimate(flops=0, bytes_accessed=2 * nbytes, transcendentals=0),
+        name="stage",
+    )(from_hbm(w_up), payload)
+
+
+def collect_kernel(staged, *refs):
+    del staged
+    for i, ref in enumerate(refs[:-1]):
+        refs[-1][i] = ref[...]
+
+
+def collect(staged, pieces):
+    first = pieces[0]
+    return pl.pallas_call(
+        collect_kernel,
+        out_shape=VMEM((len(pieces),) + first.shape, first.dtype),
+        in_specs=in_vmem(1 + len(pieces)),
+        out_specs=pl.BlockSpec(memory_space=VMEM),
+        compiler_params=pltpu.CompilerParams(vmem_limit_bytes=4 * MIB),
+        name="collect",
+    )(*[pltpu.with_memory_space_constraint(a, VMEM) for a in (staged, *pieces)])
+
+
 def chunk_width(width):
-    return next(c for c in (512, 384, 256, 128) if width % c == 0)
-
-
-def expert_kernel(plan, n_early, n_out, placement, router, w_up, w_down, *refs):
+    return next(c for c in (768, 512, 384, 256, 128) if width % c == 0)
+
+
+def expert_kernel(plan, n_staged, n_out, placement, router, w_up, w_down, *refs):
     pieces, places, halves, relative, n_slots = plan
     piece_refs, refs = refs[:pieces], refs[pieces:]
-    early_refs, refs = refs[: n_early > 0], refs[n_early > 0 :]
+    early_refs, refs = refs[: n_staged], refs[n_staged:]
     out_refs, refs = refs[:n_out], refs[n_out:]
-    state, hidden, flat, late, ring, late_sems, ring_sems = refs
+    state, hidden, sums, ring, ring_sems = refs
     rows, width = state.shape
     slice_width = width // halves
     total_units = w_up.shape[0]
@@ -156,29 +195,21 @@
     def half_start(half):
         return pl.multiple_of((tp ^ half if relative else half) * slice_width, LANES)
 
-    def fetch(i):
+    held = [(ref, at) for ref in early_refs for at in range(0, ref.shape[0], units)]
+    n_late = local_experts - len(held)
+    blocks = n_late + local_experts
+
+    def load(i):
+        source, at = (w_up, len(held) + i) if i < n_late else (w_down, i - n_late)
         return pltpu.make_async_copy(
-            w_up.at[pl.ds(n_early + i * units, units)],
-            late.at[pl.ds(i * units, units)],
-            late_sems.at[i],
+            source.at[pl.ds(at * units, units)], ring.at[i % n_slots], ring_sems.at[i % n_slots]
         )
 
-    n_late = late.shape[0] // units
-    for i in range(n_late):
-        fetch(i).start()
-    step = ring.shape[2]
-    per_half = slice_width // step
-    chunks = halves * per_half
-
-    def load(i):
-        half = halves - 1 - i // per_half
-        start = pl.multiple_of(half_start(half) + (i % per_half) * step, LANES)
-        slot = i % n_slots
-        return pltpu.make_async_copy(
-            w_down.at[:, pl.ds(start, step)], ring.at[slot], ring_sems.at[slot]
-        )
-
-    for i in range(min(n_slots, chunks)):
+    def next_load(i):
+        if i + n_slots < blocks:
+            load(i + n_slots).start()
+
+    for i in range(min(n_slots, blocks)):
         load(i).start()
 
     picks = [None] * (rows // 16)
@@ -205,11 +236,11 @@
         gate = jnp.zeros((1, rows), jnp.float32)
         for e in range(experts):
             gate = jnp.where(placement[e] == ae * local_experts + p, gates[e : e + 1], gate)
-        if p * units < n_early:
-            weights, base = early_refs[0], p * units
+        if p < len(held):
+            weights, base = held[p]
         else:
-            weights, base = late, p * units - n_early
-            fetch(base // units).wait()
+            weights, base = ring.at[(p - len(held)) % n_slots], 0
+            load(p - len(held)).wait()
         for start in range(0, units, span):
             up = lax.dot_general(
                 weights[base + start : base + start + span],
@@ -221,41 +252,53 @@
             act = up / (1.0 + jnp.exp(-up)) * gate
             at = p * units + start
             hidden[at : at + span, :] = act.astype(jnp.bfloat16)
-    flat[...] = hidden[...].T
+        if p >= len(held):
+            next_load(p - len(held))
 
     shares = rows // n_out
-    for i in range(chunks):
+    step = chunk_width(slice_width)
+    for p in range(local_experts):
+        i = n_late + p
         load(i).wait()
-        half, at = halves - 1 - i // per_half, (i % per_half) * step
-        total = jnp.dot(flat[...], ring[i % n_slots], preferred_element_type=jnp.float32)
-        if i + n_slots < chunks:
-            load(i + n_slots).start()
-        for n, out in enumerate(out_refs):
-            out[half, :, at : at + step] = total[n * shares : (n + 1) * shares].astype(out.dtype)
+        for half in range(halves):
+            for at in range(0, slice_width, step):
+                start = pl.multiple_of(half_start(half) + at, LANES)
+                total = lax.dot_general(
+                    hidden[p * units : (p + 1) * units],
+                    ring[i % n_slots, :, pl.ds(start, step)],
+                    TN,
+                    preferred_element_type=jnp.float32,
+                )
+                if p > 0:
+                    total = total + sums[half, :, at : at + step]
+                if p < local_experts - 1:
+                    sums[half, :, at : at + step] = total
+                    continue
+                for n, out in enumerate(out_refs):
+                    share = total[n * shares : (n + 1) * shares]
+                    out[half, :, at : at + step] = share.astype(out.dtype)
+        next_load(i)
 
 
 def up_span(units):
     return 336 if units % 336 == 0 else units
 
 
-def run_experts(plan, n_early, out_types, placement, router, w_up, w_down, pieces, early, rows):
+def run_experts(plan, out_types, placement, router, w_up, w_down, pieces, early, rows):
     halves = plan[2]
     total_units, width = w_up.shape
     local_experts = router.shape[0] // lax.axis_size("ae")
     units = total_units // local_experts
-    step = chunk_width(width // halves)
     n_out = len(out_types)
     scratch = [
         VMEM((rows, width), jnp.bfloat16),
         VMEM((total_units, rows), jnp.bfloat16),
-        VMEM((rows, total_units), jnp.bfloat16),
-        VMEM((total_units - n_early, width), jnp.bfloat16),
-        VMEM((plan[4], total_units, step), jnp.bfloat16),
-        pltpu.SemaphoreType.DMA(((total_units - n_early) // units,)),
+        VMEM((halves, rows, width // halves), jnp.float32),
+        VMEM((plan[4], units, width), jnp.bfloat16),
         pltpu.SemaphoreType.DMA((plan[4],)),
     ]
     return pl.pallas_call(
-        functools.partial(expert_kernel, plan, n_early, n_out),
+        functools.partial(expert_kernel, plan, len(early), n_out),
         out_shape=[VMEM((halves, rows // n_out, width // halves), t) for t in out_types],
         in_specs=[pl.BlockSpec(memory_space=pltpu.SMEM)]
         + in_vmem(1)
@@ -263,7 +306,7 @@
         + in_vmem(len(pieces) + len(early)),
         out_specs=in_vmem(n_out),
         scratch_shapes=scratch,
-        compiler_params=pltpu.CompilerParams(vmem_limit_bytes=50 * MIB),
+        compiler_params=pltpu.CompilerParams(vmem_limit_bytes=38 * MIB),
         name="experts",
     )(
         placement,
@@ -337,14 +380,14 @@
         n_early, tokens, queries, kv_cache, new_kv, lengths, routes, w_up
     )
 
-    direct = n_tp == 2 and n_sub == 2 and n_ae in (2, 4) and row_count == 16
+    direct = n_tp == 2 and n_sub == 2 and n_ae == 4 and row_count == 16
     if not direct:
         pieces = [lax.all_gather(payload, ("ae", "sub", "tp"), axis=0)]
         blocks = n_ae * n_sub
         places = [[(b * n_tp + t, b, t) for b in range(blocks) for t in range(n_tp)]]
         plan = (1, places, n_tp, False, 2)
         (total,) = run_experts(
-            plan, n_early, [jnp.float32], placement, router, w_up, w_down, pieces, early, rows
+            plan, [jnp.float32], placement, router, w_up, w_down, pieces, early, rows
         )
         total = total.reshape(n_tp, blocks, row_count, slice_width).swapaxes(0, 1)
         total = lax.psum_scatter(
@@ -369,12 +412,17 @@
 
     partners = [(da, dt) for da in range(n_ae) for dt in range(n_tp)]
     near = [payload] + [swap(payload, da, dt, 0) for da, dt in partners[1:]]
-    pieces = near + [swap(piece, 0, 0, 1) for piece in near]
-    places = [[(None, ds * n_ae + da, dt)] for ds in range(n_sub) for da, dt in partners]
+    staged = stage(n_early, local_experts // 4 * units, w_up, payload)
+    near = collect(staged, near)
+    pieces = [near, swap(near, 0, 0, 1)]
+    early.append(staged)
+    places = [
+        [(i, ds * n_ae + da, dt) for i, (da, dt) in enumerate(partners)] for ds in range(n_sub)
+    ]
     plan = (len(pieces), places, n_tp, True, 4)
     types = [jnp.float32, jnp.bfloat16]
     mine, other = run_experts(
-        plan, n_early, types, placement, router, w_up, w_down, pieces, early, rows
+        plan, types, placement, router, w_up, w_down, pieces, early, rows
     )
     kept, *sent = pair_sum(mine, swap(other, 0, 0, 1))
     received = [swap(part, da, dt, 0) for part, (da, dt) in zip(sent, partners[1:])]

time: 66.9 us -> 62.3 us (0.931)
  waiting for transfers between devices: 12.3 us -> 10.1 us
  starting transfers between devices: 25.3 us -> 24 us
  Pallas kernels: 28.4 us -> 27.2 us
    ppermute x23 -> x16, waiting for transfers between devices: 12.3 us -> 10.1 us  [swap(): return lax.ppermute(value, ('ae', 'tp', 'sub'), pairs)]
    ppermute x23 -> x16, starting transfers between devices: 25.3 us -> 24 us  [swap(): return lax.ppermute(value, ('ae', 'tp', 'sub'), pairs)]
    pallas_call x1 -> x3, Pallas kernels: 23.6 us -> 22.3 us  [the longest x1 18.9 us: run_experts(): pl.pallas_call(functools.partial(expert_kernel, plan, len(early), n_out),...]
  transfers between devices with their start and end apart: 23 -> 16, of which waited for: 12 -> 5; matrix products, arithmetic and copies ran while one was open for 0% -> 0% of each run, Pallas kernels for 0% -> 5%
where the time goes in v3:
time: 62.3 us; the launch traced here: 62.2 us
  Pallas kernels  27.2 us (44%)
  starting transfers between devices  24 us (39%)
  waiting for transfers between devices  10.1 us (16%)
  local copies, waits for them, and re-layouts  0.75 us (1%)
    ppermute x16, starting transfers between devices, swap(): return lax.ppermute(value, ('ae', 'tp', 'sub'), pairs)  24 us
    pallas_call x1, Pallas kernels, run_experts(): pl.pallas_call(functools.partial(expert_kernel, plan, len(early), n_out),...  18.9 us
    ppermute x16, waiting for transfers between devices, swap(): return lax.ppermute(value, ('ae', 'tp', 'sub'), pairs)  10.1 us
    pallas_call x1, Pallas kernels, attend(): pl.pallas_call(functools.partial(attention_kernel, n_early), out_shape=ou...  4.15 us
    pallas_call x1, Pallas kernels, stage(): pl.pallas_call(functools.partial(stage_kernel, start), out_shape=VMEM((co...  3.35 us
  transfers between devices with their start and end apart: 16, of which 5 were waited for; matrix products, arithmetic and copies ran while one was open for 0% of the time, Pallas kernels for 5%

profile of v3, /device:TPU:0, one launch (start us, length us, event | category | flops | bytes accessed | tf_op | source)
XLA Modules:
  0.0 62.2 jit_solution(3278993595412890674)
XLA Ops:
  0.0 4.1 %attention.1 = (bf16[16,1664]{1,0:T(8,128)(2,1)S(1)}, bf16[1344,3072]{1,0:T(8,128)(2,1)S(1)}) custom-call(bf16[2,16,4,64,128]{4,3,2,1,0:T(8,128)(2,1)} %refs_0_.1, bf16[16,1536]{1,0:T(8,128)(2,1)} %refs_1_.1, bf16[2,16,512]{2,1,0:T(8,128)(2,1)} %refs_2_.1, bf16[16,1536]{1,0:T(8,128)(2,1)} %refs_3_.1, s32[1,16]{1,0:T(1,128)} %bitcast.13, s32[4,16]{1,0:T(4,128)} %bitcast.12, ...), custom_call_target="tpu_custom_call" | custom-call | tf_op jit(solution)/shard_map/attention/pallas_call | solution.py:122
  4.2 6.0 %collective-permute-start.6 = (bf16[16,1664]{1,0:T(8,128)(2,1)S(1)}, bf16[16,1664]{1,0:T(8,128)(2,1)S(1)}, u32[]{:S(2)}, u32[]{:S(2)}) collective-permute-start(bf16[16,1664]{1,0:T(8,128)(2,1)S(1)} %get-tuple-element.17.payload.refs_0_), channel_id=1, source_target_pairs={{0,14},{1,15},{2,12},{3,13},{4,10},{5,11},{6,8},{7,9},{8,6},{9,7},... | collective-permute-start | bytes 159752 | tf_op jit(solution)/shard_map/ppermute | solution.py:411
  10.2 0.2 collective-permute-start.5
  10.4 0.8 %collective-permute-start.4 = (bf16[16,1664]{1,0:T(8,128)(2,1)S(1)}, bf16[16,1664]{1,0:T(8,128)(2,1)S(1)}, u32[]{:S(2)}, u32[]{:S(2)}) collective-permute-start(bf16[16,1664]{1,0:T(8,128)(2,1)S(1)} %get-tuple-element.17.payload.refs_0_), channel_id=1, source_target_pairs={{0,10},{1,11},{2,8},{3,9},{4,14},{5,15},{6,12},{7,13},{8,2},{9,3},... | collective-permute-start | bytes 159752 | tf_op jit(solution)/shard_map/ppermute | solution.py:411
  11.2 2.0 %collective-permute-start.3 = (bf16[16,1664]{1,0:T(8,128)(2,1)S(1)}, bf16[16,1664]{1,0:T(8,128)(2,1)S(1)}, u32[]{:S(2)}, u32[]{:S(2)}) collective-permute-start(bf16[16,1664]{1,0:T(8,128)(2,1)S(1)} %get-tuple-element.17.payload.refs_0_), channel_id=1, source_target_pairs={{0,8},{1,9},{2,10},{3,11},{4,12},{5,13},{6,14},{7,15},{8,0},{9,1},... | collective-permute-start | bytes 159752 | tf_op jit(solution)/shard_map/ppermute | solution.py:411
  13.2 2.3 %collective-permute-start.2 = (bf16[16,1664]{1,0:T(8,128)(2,1)S(1)}, bf16[16,1664]{1,0:T(8,128)(2,1)S(1)}, u32[]{:S(2)}, u32[]{:S(2)}) collective-permute-start(bf16[16,1664]{1,0:T(8,128)(2,1)S(1)} %get-tuple-element.17.payload.refs_0_), channel_id=1, source_target_pairs={{0,6},{1,7},{2,4},{3,5},{4,2},{5,3},{6,0},{7,1},{8,14},{9,15},{10,... | collective-permute-start | bytes 159752 | tf_op jit(solution)/shard_map/ppermute | solution.py:411
  15.5 0.8 %collective-permute-start.1 = (bf16[16,1664]{1,0:T(8,128)(2,1)S(1)}, bf16[16,1664]{1,0:T(8,128)(2,1)S(1)}, u32[]{:S(2)}, u32[]{:S(2)}) collective-permute-start(bf16[16,1664]{1,0:T(8,128)(2,1)S(1)} %get-tuple-element.17.payload.refs_0_), channel_id=1, source_target_pairs={{0,4},{1,5},{2,6},{3,7},{4,0},{5,1},{6,2},{7,3},{8,12},{9,13},{10,... | collective-permute-start | bytes 159752 | tf_op jit(solution)/shard_map/ppermute | solution.py:411
  16.3 0.4 collective-permute-start
  16.7 3.4 %stage.1.staged.refs_3_ = bf16[1344,3072]{1,0:T(8,128)(2,1)S(1)} custom-call(bf16[5376,3072]{1,0:T(8,128)(2,1)} %bitcast.8, bf16[16,1664]{1,0:T(8,128)(2,1)S(1)} %get-tuple-element.17.payload.refs_0_), custom_call_target="tpu_custom_call" | custom-call | bytes 16515072 | tf_op jit(solution)/shard_map/stage/pallas_call | solution.py:146
  20.1 0.3 collective-permute-done.refs_1_
  20.5 1.8 %collective-permute-done.7.refs_1_ = bf16[8,16,1664]{2,1,0:T(8,128)(2,1)S(1)} collective-permute-done((bf16[8,16,1664]{2,1,0:T(8,128)(2,1)S(1)}, bf16[8,16,1664]{2,1,0:T(8,128)(2,1)S(1)}, u32[]{:S(2)}, u32[]{:S(2)}) %collective-permute-start.7) | collective-permute-done | bytes 426016 | tf_op jit(solution)/shard_map/ppermute | solution.py:411
  22.3 0.7 %copy-done.1 = bf16[8,16,1664]{2,1,0:T(8,128)(2,1)} copy-done((bf16[8,16,1664]{2,1,0:T(8,128)(2,1)}, bf16[8,16,1664]{2,1,0:T(8,128)(2,1)S(1)}, u32[]{:S(2)}) %copy-start.1) | copy-done | bytes 426008
  23.0 18.9 %experts.1 = (f32[2,64,1536]{2,1,0:T(8,128)S(1)}, bf16[2,64,1536]{2,1,0:T(8,128)(2,1)S(1)}) custom-call(s32[16]{0:T(128)} %placement.1, bf16[16,3072]{1,0:T(8,128)(2,1)} %bitcast.11, bf16[5376,3072]{1,0:T(8,128)(2,1)} %bitcast.9, bf16[5376,3072]{1,0:T(8,128)(2,1)} %bitcast.10, bf16[8,16,1664]{2,1,0:T(8,128)(2,1)} %copy-done, bf16[8,16,1664]{2,1,0:T(8,128)(2,1)} %copy-done.1, ...), custom_call_target="tpu_custom_call" | custom-call | tf_op jit(solution)/shard_map/experts/pallas_call | solution.py:300
  42.2 1.6 %collective-permute-done.8.other = bf16[2,64,1536]{2,1,0:T(8,128)(2,1)S(1)} collective-permute-done((bf16[2,64,1536]{2,1,0:T(8,128)(2,1)S(1)}, bf16[2,64,1536]{2,1,0:T(8,128)(2,1)S(1)}, u32[]{:S(2)}, u32[]{:S(2)}) %collective-permute-start.8) | collective-permute-done | bytes 393248 | tf_op jit(solution)/shard_map/ppermute | solution.py:411
  43.9 1.4 %collective-permute-start.9 = (bf16[16,1536]{1,0:T(8,128)(2,1)S(1)}, bf16[16,1536]{1,0:T(8,128)(2,1)S(1)}, u32[]{:S(2)}, u32[]{:S(2)}) collective-permute-start(bf16[16,1536]{1,0:T(8,128)(2,1)S(1)} %get-tuple-element.22), channel_id=1, source_target_pairs={{0,2},{1,3},{2,0},{3,1},{4,6},{5,7},{6,4},{7,5},{8,10},{9,11},{10,... | collective-permute-start | bytes 147464 | tf_op jit(solution)/shard_map/ppermute | solution.py:411
  45.2 1.2 %collective-permute-start.10 = (bf16[16,1536]{1,0:T(8,128)(2,1)S(1)}, bf16[16,1536]{1,0:T(8,128)(2,1)S(1)}, u32[]{:S(2)}, u32[]{:S(2)}) collective-permute-start(bf16[16,1536]{1,0:T(8,128)(2,1)S(1)} %get-tuple-element.23), channel_id=1, source_target_pairs={{0,4},{1,5},{2,6},{3,7},{4,0},{5,1},{6,2},{7,3},{8,12},{9,13},{10,... | collective-permute-start | bytes 147464 | tf_op jit(solution)/shard_map/ppermute | solution.py:411
  46.5 0.9 %collective-permute-start.11 = (bf16[16,1536]{1,0:T(8,128)(2,1)S(1)}, bf16[16,1536]{1,0:T(8,128)(2,1)S(1)}, u32[]{:S(2)}, u32[]{:S(2)}) collective-permute-start(bf16[16,1536]{1,0:T(8,128)(2,1)S(1)} %get-tuple-element.24), channel_id=1, source_target_pairs={{0,6},{1,7},{2,4},{3,5},{4,2},{5,3},{6,0},{7,1},{8,14},{9,15},{10,... | collective-permute-start | bytes 147464 | tf_op jit(solution)/shard_map/ppermute | solution.py:411
  47.4 2.4 %collective-permute-start.12 = (bf16[16,1536]{1,0:T(8,128)(2,1)S(1)}, bf16[16,1536]{1,0:T(8,128)(2,1)S(1)}, u32[]{:S(2)}, u32[]{:S(2)}) collective-permute-start(bf16[16,1536]{1,0:T(8,128)(2,1)S(1)} %get-tuple-element.25), channel_id=1, source_target_pairs={{0,8},{1,9},{2,10},{3,11},{4,12},{5,13},{6,14},{7,15},{8,0},{9,1},... | collective-permute-start | bytes 147464 | tf_op jit(solution)/shard_map/ppermute | solution.py:411
  49.8 1.3 %collective-permute-start.13 = (bf16[16,1536]{1,0:T(8,128)(2,1)S(1)}, bf16[16,1536]{1,0:T(8,128)(2,1)S(1)}, u32[]{:S(2)}, u32[]{:S(2)}) collective-permute-start(bf16[16,1536]{1,0:T(8,128)(2,1)S(1)} %get-tuple-element.26), channel_id=1, source_target_pairs={{0,10},{1,11},{2,8},{3,9},{4,14},{5,15},{6,12},{7,13},{8,2},{9,3},... | collective-permute-start | bytes 147464 | tf_op jit(solution)/shard_map/ppermute | solution.py:411
  51.1 3.6 %collective-permute-start.14 = (bf16[16,1536]{1,0:T(8,128)(2,1)S(1)}, bf16[16,1536]{1,0:T(8,128)(2,1)S(1)}, u32[]{:S(2)}, u32[]{:S(2)}) collective-permute-start(bf16[16,1536]{1,0:T(8,128)(2,1)S(1)} %get-tuple-element.27), channel_id=1, source_target_pairs={{0,12},{1,13},{2,14},{3,15},{4,8},{5,9},{6,10},{7,11},{8,4},{9,5},... | collective-permute-start | bytes 147464 | tf_op jit(solution)/shard_map/ppermute | solution.py:411
  54.7 0.4 collective-permute-start.15
  55.1 2.6 %collective-permute-done.13.refs_4_ = bf16[16,1536]{1,0:T(8,128)(2,1)S(1)} collective-permute-done((bf16[16,1536]{1,0:T(8,128)(2,1)S(1)}, bf16[16,1536]{1,0:T(8,128)(2,1)S(1)}, u32[]{:S(2)}, u32[]{:S(2)}) %collective-permute-start.13) | collective-permute-done | bytes 49184 | tf_op jit(solution)/shard_map/ppermute | solution.py:411
  57.7 3.8 %collective-permute-done.15.refs_6_ = bf16[16,1536]{1,0:T(8,128)(2,1)S(1)} collective-permute-done((bf16[16,1536]{1,0:T(8,128)(2,1)S(1)}, bf16[16,1536]{1,0:T(8,128)(2,1)S(1)}, u32[]{:S(2)}, u32[]{:S(2)}) %collective-permute-start.15) | collective-permute-done | bytes 49184 | tf_op jit(solution)/shard_map/ppermute | solution.py:411
  61.5 0.7 %chip_sum.1 = bf16[16,1536]{1,0:T(8,128)(2,1)} custom-call(f32[16,1536]{1,0:T(8,128)S(1)} %get-tuple-element.21.kept, bf16[16,1536]{1,0:T(8,128)(2,1)S(1)} %collective-permute-done.9.refs_0_, bf16[16,1536]{1,0:T(8,128)(2,1)S(1)} %collective-permute-done.10.refs_1_, bf16[16,1536]{1,0:T(8,128)(2,1)S(1)} %collective-permute-done.11.refs_2_, ...), custom_call_target="tpu_custom_call" | custom-call | tf_op jit(solution)/shard_map/chip_sum/pallas_call | solution.py:357
  (18 shorter events, 0.4 us)
Async XLA Ops:
  4.2 11.3 %collective-permute-start.6 = (bf16[16,1664]{1,0:T(8,128)(2,1)S(1)}, bf16[16,1664]{1,0:T(8,128)(2,1)S(1)}, u32[]{:S(2)}, u32[]{:S(2)}) collective-permute-start(bf16[16,1664]{1,0:T(8,128)(2,1)S(1)} %get-tuple-element.17.payload.refs_0_), channel_id=1, source_target_pairs={{0,14},{1,15},{2,12},{3,13},{4,10},{5,11},{6,8},{7,9},{8,6},{9,7},... | collective-permute-start | bytes 159752 | tf_op jit(solution)/shard_map/ppermute | solution.py:411
  10.2 6.1 %collective-permute-start.5 = (bf16[16,1664]{1,0:T(8,128)(2,1)S(1)}, bf16[16,1664]{1,0:T(8,128)(2,1)S(1)}, u32[]{:S(2)}, u32[]{:S(2)}) collective-permute-start(bf16[16,1664]{1,0:T(8,128)(2,1)S(1)} %get-tuple-element.17.payload.refs_0_), channel_id=1, source_target_pairs={{0,12},{1,13},{2,14},{3,15},{4,8},{5,9},{6,10},{7,11},{8,4},{9,5},... | collective-permute-start | bytes 159752 | tf_op jit(solution)/shard_map/ppermute | solution.py:411
  10.4 9.7 %collective-permute-start.4 = (bf16[16,1664]{1,0:T(8,128)(2,1)S(1)}, bf16[16,1664]{1,0:T(8,128)(2,1)S(1)}, u32[]{:S(2)}, u32[]{:S(2)}) collective-permute-start(bf16[16,1664]{1,0:T(8,128)(2,1)S(1)} %get-tuple-element.17.payload.refs_0_), channel_id=1, source_target_pairs={{0,10},{1,11},{2,8},{3,9},{4,14},{5,15},{6,12},{7,13},{8,2},{9,3},... | collective-permute-start | bytes 159752 | tf_op jit(solution)/shard_map/ppermute | solution.py:411
  11.2 8.9 %collective-permute-start.3 = (bf16[16,1664]{1,0:T(8,128)(2,1)S(1)}, bf16[16,1664]{1,0:T(8,128)(2,1)S(1)}, u32[]{:S(2)}, u32[]{:S(2)}) collective-permute-start(bf16[16,1664]{1,0:T(8,128)(2,1)S(1)} %get-tuple-element.17.payload.refs_0_), channel_id=1, source_target_pairs={{0,8},{1,9},{2,10},{3,11},{4,12},{5,13},{6,14},{7,15},{8,0},{9,1},... | collective-permute-start | bytes 159752 | tf_op jit(solution)/shard_map/ppermute | solution.py:411
  13.2 6.9 %collective-permute-start.2 = (bf16[16,1664]{1,0:T(8,128)(2,1)S(1)}, bf16[16,1664]{1,0:T(8,128)(2,1)S(1)}, u32[]{:S(2)}, u32[]{:S(2)}) collective-permute-start(bf16[16,1664]{1,0:T(8,128)(2,1)S(1)} %get-tuple-element.17.payload.refs_0_), channel_id=1, source_target_pairs={{0,6},{1,7},{2,4},{3,5},{4,2},{5,3},{6,0},{7,1},{8,14},{9,15},{10,... | collective-permute-start | bytes 159752 | tf_op jit(solution)/shard_map/ppermute | solution.py:411
  15.5 4.6 %collective-permute-start.1 = (bf16[16,1664]{1,0:T(8,128)(2,1)S(1)}, bf16[16,1664]{1,0:T(8,128)(2,1)S(1)}, u32[]{:S(2)}, u32[]{:S(2)}) collective-permute-start(bf16[16,1664]{1,0:T(8,128)(2,1)S(1)} %get-tuple-element.17.payload.refs_0_), channel_id=1, source_target_pairs={{0,4},{1,5},{2,6},{3,7},{4,0},{5,1},{6,2},{7,3},{8,12},{9,13},{10,... | collective-permute-start | bytes 159752 | tf_op jit(solution)/shard_map/ppermute | solution.py:411
  16.3 4.1 %collective-permute-start = (bf16[16,1664]{1,0:T(8,128)(2,1)S(1)}, bf16[16,1664]{1,0:T(8,128)(2,1)S(1)}, u32[]{:S(2)}, u32[]{:S(2)}) collective-permute-start(bf16[16,1664]{1,0:T(8,128)(2,1)S(1)} %get-tuple-element.17.payload.refs_0_), channel_id=1, source_target_pairs={{0,2},{1,3},{2,0},{3,1},{4,6},{5,7},{6,4},{7,5},{8,10},{9,11},{10,... | collective-permute-start | bytes 159752 | tf_op jit(solution)/shard_map/ppermute | solution.py:411
  20.4 1.9 %copy-start = (bf16[8,16,1664]{2,1,0:T(8,128)(2,1)}, bf16[8,16,1664]{2,1,0:T(8,128)(2,1)S(1)}, u32[]{:S(2)}) copy-start(bf16[8,16,1664]{2,1,0:T(8,128)(2,1)S(1)} %collect.1.refs_0_) | copy-start | bytes 1277956
  20.5 1.8 %collective-permute-start.7 = (bf16[8,16,1664]{2,1,0:T(8,128)(2,1)S(1)}, bf16[8,16,1664]{2,1,0:T(8,128)(2,1)S(1)}, u32[]{:S(2)}, u32[]{:S(2)}) collective-permute-start(bf16[8,16,1664]{2,1,0:T(8,128)(2,1)S(1)} %collect.1.refs_0_), channel_id=1, source_target_pairs={{0,1},{1,0},{2,3},{3,2},{4,5},{5,4},{6,7},{7,6},{8,9},{9,8},{10,11... | collective-permute-start | bytes 1277960 | tf_op jit(solution)/shard_map/ppermute | solution.py:411
  22.3 0.8 %copy-start.1 = (bf16[8,16,1664]{2,1,0:T(8,128)(2,1)}, bf16[8,16,1664]{2,1,0:T(8,128)(2,1)S(1)}, u32[]{:S(2)}) copy-start(bf16[8,16,1664]{2,1,0:T(8,128)(2,1)S(1)} %collective-permute-done.7.refs_1_) | copy-start | bytes 1277956
  42.0 1.8 %collective-permute-start.8 = (bf16[2,64,1536]{2,1,0:T(8,128)(2,1)S(1)}, bf16[2,64,1536]{2,1,0:T(8,128)(2,1)S(1)}, u32[]{:S(2)}, u32[]{:S(2)}) collective-permute-start(bf16[2,64,1536]{2,1,0:T(8,128)(2,1)S(1)} %get-tuple-element.20), channel_id=1, source_target_pairs={{0,1},{1,0},{2,3},{3,2},{4,5},{5,4},{6,7},{7,6},{8,9},{9,8},{10,11... | collective-permute-start | bytes 1179656 | tf_op jit(solution)/shard_map/ppermute | solution.py:411
  43.9 7.2 %collective-permute-start.9 = (bf16[16,1536]{1,0:T(8,128)(2,1)S(1)}, bf16[16,1536]{1,0:T(8,128)(2,1)S(1)}, u32[]{:S(2)}, u32[]{:S(2)}) collective-permute-start(bf16[16,1536]{1,0:T(8,128)(2,1)S(1)} %get-tuple-element.22), channel_id=1, source_target_pairs={{0,2},{1,3},{2,0},{3,1},{4,6},{5,7},{6,4},{7,5},{8,10},{9,11},{10,... | collective-permute-start | bytes 147464 | tf_op jit(solution)/shard_map/ppermute | solution.py:411
  45.2 9.5 %collective-permute-start.10 = (bf16[16,1536]{1,0:T(8,128)(2,1)S(1)}, bf16[16,1536]{1,0:T(8,128)(2,1)S(1)}, u32[]{:S(2)}, u32[]{:S(2)}) collective-permute-start(bf16[16,1536]{1,0:T(8,128)(2,1)S(1)} %get-tuple-element.23), channel_id=1, source_target_pairs={{0,4},{1,5},{2,6},{3,7},{4,0},{5,1},{6,2},{7,3},{8,12},{9,13},{10,... | collective-permute-start | bytes 147464 | tf_op jit(solution)/shard_map/ppermute | solution.py:411
  46.5 8.6 %collective-permute-start.11 = (bf16[16,1536]{1,0:T(8,128)(2,1)S(1)}, bf16[16,1536]{1,0:T(8,128)(2,1)S(1)}, u32[]{:S(2)}, u32[]{:S(2)}) collective-permute-start(bf16[16,1536]{1,0:T(8,128)(2,1)S(1)} %get-tuple-element.24), channel_id=1, source_target_pairs={{0,6},{1,7},{2,4},{3,5},{4,2},{5,3},{6,0},{7,1},{8,14},{9,15},{10,... | collective-permute-start | bytes 147464 | tf_op jit(solution)/shard_map/ppermute | solution.py:411
  47.4 7.7 %collective-permute-start.12 = (bf16[16,1536]{1,0:T(8,128)(2,1)S(1)}, bf16[16,1536]{1,0:T(8,128)(2,1)S(1)}, u32[]{:S(2)}, u32[]{:S(2)}) collective-permute-start(bf16[16,1536]{1,0:T(8,128)(2,1)S(1)} %get-tuple-element.25), channel_id=1, source_target_pairs={{0,8},{1,9},{2,10},{3,11},{4,12},{5,13},{6,14},{7,15},{8,0},{9,1},... | collective-permute-start | bytes 147464 | tf_op jit(solution)/shard_map/ppermute | solution.py:411
  49.8 7.9 %collective-permute-start.13 = (bf16[16,1536]{1,0:T(8,128)(2,1)S(1)}, bf16[16,1536]{1,0:T(8,128)(2,1)S(1)}, u32[]{:S(2)}, u32[]{:S(2)}) collective-permute-start(bf16[16,1536]{1,0:T(8,128)(2,1)S(1)} %get-tuple-element.26), channel_id=1, source_target_pairs={{0,10},{1,11},{2,8},{3,9},{4,14},{5,15},{6,12},{7,13},{8,2},{9,3},... | collective-permute-start | bytes 147464 | tf_op jit(solution)/shard_map/ppermute | solution.py:411
  51.1 6.6 %collective-permute-start.14 = (bf16[16,1536]{1,0:T(8,128)(2,1)S(1)}, bf16[16,1536]{1,0:T(8,128)(2,1)S(1)}, u32[]{:S(2)}, u32[]{:S(2)}) collective-permute-start(bf16[16,1536]{1,0:T(8,128)(2,1)S(1)} %get-tuple-element.27), channel_id=1, source_target_pairs={{0,12},{1,13},{2,14},{3,15},{4,8},{5,9},{6,10},{7,11},{8,4},{9,5},... | collective-permute-start | bytes 147464 | tf_op jit(solution)/shard_map/ppermute | solution.py:411
  54.7 6.8 %collective-permute-start.15 = (bf16[16,1536]{1,0:T(8,128)(2,1)S(1)}, bf16[16,1536]{1,0:T(8,128)(2,1)S(1)}, u32[]{:S(2)}, u32[]{:S(2)}) collective-permute-start(bf16[16,1536]{1,0:T(8,128)(2,1)S(1)} %get-tuple-element.28), channel_id=1, source_target_pairs={{0,14},{1,15},{2,12},{3,13},{4,10},{5,11},{6,8},{7,9},{8,6},{9,7},... | collective-permute-start | bytes 147464 | tf_op jit(solution)/shard_map/ppermute | solution.py:411

commit v4 on v3

--- a/solution.py
+++ b/solution.py
@@ -425,7 +425,7 @@
         plan, types, placement, router, w_up, w_down, pieces, early, rows
     )
     kept, *sent = pair_sum(mine, swap(other, 0, 0, 1))
-    received = [swap(part, da, dt, 0) for part, (da, dt) in zip(sent, partners[1:])]
+    received = [swap(part, da, dt, 0) for part, (da, dt) in zip(sent[::-1], partners[:0:-1])]
     return chip_sum(kept, received)
 
 

time: 62.3 us -> 59.3 us (0.952)
  waiting for transfers between devices: 10.1 us -> 7.04 us
    ppermute x16, waiting for transfers between devices: 10.1 us -> 7.04 us  [swap(): return lax.ppermute(value, ('ae', 'tp', 'sub'), pairs)]
  transfers between devices with their start and end apart: 16 -> 16, of which waited for: 5 -> 7; matrix products, arithmetic and copies ran while one was open for 0% -> 0% of each run, Pallas kernels for 5% -> 6%
where the time goes in v4:
time: 59.3 us; the launch traced here: 59.1 us
  Pallas kernels  27.2 us (46%)
  starting transfers between devices  24 us (40%)
  waiting for transfers between devices  7.04 us (12%)
  local copies, waits for them, and re-layouts  0.75 us (1%)
    ppermute x16, starting transfers between devices, swap(): return lax.ppermute(value, ('ae', 'tp', 'sub'), pairs)  24 us
    pallas_call x1, Pallas kernels, run_experts(): pl.pallas_call(functools.partial(expert_kernel, plan, len(early), n_out),...  18.9 us
    ppermute x16, waiting for transfers between devices, swap(): return lax.ppermute(value, ('ae', 'tp', 'sub'), pairs)  7.04 us
    pallas_call x1, Pallas kernels, attend(): pl.pallas_call(functools.partial(attention_kernel, n_early), out_shape=ou...  4.15 us
    pallas_call x1, Pallas kernels, stage(): pl.pallas_call(functools.partial(stage_kernel, start), out_shape=VMEM((co...  3.35 us
  transfers between devices with their start and end apart: 16, of which 7 were waited for; matrix products, arithmetic and copies ran while one was open for 0% of the time, Pallas kernels for 6%

profile of v4, /device:TPU:0, one launch (start us, length us, event | category | flops | bytes accessed | tf_op | source)
XLA Modules:
  0.0 59.1 jit_solution(15799523895192155371)
XLA Ops:
  0.0 4.1 %attention.1 = (bf16[16,1664]{1,0:T(8,128)(2,1)S(1)}, bf16[1344,3072]{1,0:T(8,128)(2,1)S(1)}) custom-call(bf16[2,16,4,64,128]{4,3,2,1,0:T(8,128)(2,1)} %refs_0_.1, bf16[16,1536]{1,0:T(8,128)(2,1)} %refs_1_.1, bf16[2,16,512]{2,1,0:T(8,128)(2,1)} %refs_2_.1, bf16[16,1536]{1,0:T(8,128)(2,1)} %refs_3_.1, s32[1,16]{1,0:T(1,128)} %bitcast.13, s32[4,16]{1,0:T(4,128)} %bitcast.12, ...), custom_call_target="tpu_custom_call" | custom-call | tf_op jit(solution)/shard_map/attention/pallas_call | solution.py:122
  4.2 6.0 %collective-permute-start.6 = (bf16[16,1664]{1,0:T(8,128)(2,1)S(1)}, bf16[16,1664]{1,0:T(8,128)(2,1)S(1)}, u32[]{:S(2)}, u32[]{:S(2)}) collective-permute-start(bf16[16,1664]{1,0:T(8,128)(2,1)S(1)} %get-tuple-element.17.payload.refs_0_), channel_id=1, source_target_pairs={{0,14},{1,15},{2,12},{3,13},{4,10},{5,11},{6,8},{7,9},{8,6},{9,7},... | collective-permute-start | bytes 159752 | tf_op jit(solution)/shard_map/ppermute | solution.py:411
  10.4 0.8 %collective-permute-start.4 = (bf16[16,1664]{1,0:T(8,128)(2,1)S(1)}, bf16[16,1664]{1,0:T(8,128)(2,1)S(1)}, u32[]{:S(2)}, u32[]{:S(2)}) collective-permute-start(bf16[16,1664]{1,0:T(8,128)(2,1)S(1)} %get-tuple-element.17.payload.refs_0_), channel_id=1, source_target_pairs={{0,10},{1,11},{2,8},{3,9},{4,14},{5,15},{6,12},{7,13},{8,2},{9,3},... | collective-permute-start | bytes 159752 | tf_op jit(solution)/shard_map/ppermute | solution.py:411
  11.2 2.0 %collective-permute-start.3 = (bf16[16,1664]{1,0:T(8,128)(2,1)S(1)}, bf16[16,1664]{1,0:T(8,128)(2,1)S(1)}, u32[]{:S(2)}, u32[]{:S(2)}) collective-permute-start(bf16[16,1664]{1,0:T(8,128)(2,1)S(1)} %get-tuple-element.17.payload.refs_0_), channel_id=1, source_target_pairs={{0,8},{1,9},{2,10},{3,11},{4,12},{5,13},{6,14},{7,15},{8,0},{9,1},... | collective-permute-start | bytes 159752 | tf_op jit(solution)/shard_map/ppermute | solution.py:411
  13.2 2.3 %collective-permute-start.2 = (bf16[16,1664]{1,0:T(8,128)(2,1)S(1)}, bf16[16,1664]{1,0:T(8,128)(2,1)S(1)}, u32[]{:S(2)}, u32[]{:S(2)}) collective-permute-start(bf16[16,1664]{1,0:T(8,128)(2,1)S(1)} %get-tuple-element.17.payload.refs_0_), channel_id=1, source_target_pairs={{0,6},{1,7},{2,4},{3,5},{4,2},{5,3},{6,0},{7,1},{8,14},{9,15},{10,... | collective-permute-start | bytes 159752 | tf_op jit(solution)/shard_map/ppermute | solution.py:411
  15.5 0.8 %collective-permute-start.1 = (bf16[16,1664]{1,0:T(8,128)(2,1)S(1)}, bf16[16,1664]{1,0:T(8,128)(2,1)S(1)}, u32[]{:S(2)}, u32[]{:S(2)}) collective-permute-start(bf16[16,1664]{1,0:T(8,128)(2,1)S(1)} %get-tuple-element.17.payload.refs_0_), channel_id=1, source_target_pairs={{0,4},{1,5},{2,6},{3,7},{4,0},{5,1},{6,2},{7,3},{8,12},{9,13},{10,... | collective-permute-start | bytes 159752 | tf_op jit(solution)/shard_map/ppermute | solution.py:411
  16.3 0.4 collective-permute-start
  16.7 3.4 %stage.1.staged.refs_3_ = bf16[1344,3072]{1,0:T(8,128)(2,1)S(1)} custom-call(bf16[5376,3072]{1,0:T(8,128)(2,1)} %bitcast.8, bf16[16,1664]{1,0:T(8,128)(2,1)S(1)} %get-tuple-element.17.payload.refs_0_), custom_call_target="tpu_custom_call" | custom-call | bytes 16515072 | tf_op jit(solution)/shard_map/stage/pallas_call | solution.py:146
  20.1 0.3 collective-permute-done.refs_1_
  20.5 1.8 %collective-permute-done.7.refs_1_ = bf16[8,16,1664]{2,1,0:T(8,128)(2,1)S(1)} collective-permute-done((bf16[8,16,1664]{2,1,0:T(8,128)(2,1)S(1)}, bf16[8,16,1664]{2,1,0:T(8,128)(2,1)S(1)}, u32[]{:S(2)}, u32[]{:S(2)}) %collective-permute-start.7) | collective-permute-done | bytes 426016 | tf_op jit(solution)/shard_map/ppermute | solution.py:411
  22.3 0.7 %copy-done.1 = bf16[8,16,1664]{2,1,0:T(8,128)(2,1)} copy-done((bf16[8,16,1664]{2,1,0:T(8,128)(2,1)}, bf16[8,16,1664]{2,1,0:T(8,128)(2,1)S(1)}, u32[]{:S(2)}) %copy-start.1) | copy-done | bytes 426008
  23.0 18.9 %experts.1 = (f32[2,64,1536]{2,1,0:T(8,128)S(1)}, bf16[2,64,1536]{2,1,0:T(8,128)(2,1)S(1)}) custom-call(s32[16]{0:T(128)} %placement.1, bf16[16,3072]{1,0:T(8,128)(2,1)} %bitcast.11, bf16[5376,3072]{1,0:T(8,128)(2,1)} %bitcast.9, bf16[5376,3072]{1,0:T(8,128)(2,1)} %bitcast.10, bf16[8,16,1664]{2,1,0:T(8,128)(2,1)} %copy-done, bf16[8,16,1664]{2,1,0:T(8,128)(2,1)} %copy-done.1, ...), custom_call_target="tpu_custom_call" | custom-call | tf_op jit(solution)/shard_map/experts/pallas_call | solution.py:300
  42.2 1.6 %collective-permute-done.8.other = bf16[2,64,1536]{2,1,0:T(8,128)(2,1)S(1)} collective-permute-done((bf16[2,64,1536]{2,1,0:T(8,128)(2,1)S(1)}, bf16[2,64,1536]{2,1,0:T(8,128)(2,1)S(1)}, u32[]{:S(2)}, u32[]{:S(2)}) %collective-permute-start.8) | collective-permute-done | bytes 393248 | tf_op jit(solution)/shard_map/ppermute | solution.py:411
  43.9 4.4 %collective-permute-start.9 = (bf16[16,1536]{1,0:T(8,128)(2,1)S(1)}, bf16[16,1536]{1,0:T(8,128)(2,1)S(1)}, u32[]{:S(2)}, u32[]{:S(2)}) collective-permute-start(bf16[16,1536]{1,0:T(8,128)(2,1)S(1)} %get-tuple-element.22), channel_id=1, source_target_pairs={{0,14},{1,15},{2,12},{3,13},{4,10},{5,11},{6,8},{7,9},{8,6},{9,7},... | collective-permute-start | bytes 147464 | tf_op jit(solution)/shard_map/ppermute | solution.py:411
  48.3 0.2 collective-permute-start.10
  48.5 0.7 %collective-permute-start.11 = (bf16[16,1536]{1,0:T(8,128)(2,1)S(1)}, bf16[16,1536]{1,0:T(8,128)(2,1)S(1)}, u32[]{:S(2)}, u32[]{:S(2)}) collective-permute-start(bf16[16,1536]{1,0:T(8,128)(2,1)S(1)} %get-tuple-element.24), channel_id=1, source_target_pairs={{0,10},{1,11},{2,8},{3,9},{4,14},{5,15},{6,12},{7,13},{8,2},{9,3},... | collective-permute-start | bytes 147464 | tf_op jit(solution)/shard_map/ppermute | solution.py:411
  49.2 2.3 %collective-permute-start.12 = (bf16[16,1536]{1,0:T(8,128)(2,1)S(1)}, bf16[16,1536]{1,0:T(8,128)(2,1)S(1)}, u32[]{:S(2)}, u32[]{:S(2)}) collective-permute-start(bf16[16,1536]{1,0:T(8,128)(2,1)S(1)} %get-tuple-element.25), channel_id=1, source_target_pairs={{0,8},{1,9},{2,10},{3,11},{4,12},{5,13},{6,14},{7,15},{8,0},{9,1},... | collective-permute-start | bytes 147464 | tf_op jit(solution)/shard_map/ppermute | solution.py:411
  51.6 2.0 %collective-permute-start.13 = (bf16[16,1536]{1,0:T(8,128)(2,1)S(1)}, bf16[16,1536]{1,0:T(8,128)(2,1)S(1)}, u32[]{:S(2)}, u32[]{:S(2)}) collective-permute-start(bf16[16,1536]{1,0:T(8,128)(2,1)S(1)} %get-tuple-element.26), channel_id=1, source_target_pairs={{0,6},{1,7},{2,4},{3,5},{4,2},{5,3},{6,0},{7,1},{8,14},{9,15},{10,... | collective-permute-start | bytes 147464 | tf_op jit(solution)/shard_map/ppermute | solution.py:411
  53.6 0.8 %collective-permute-start.14 = (bf16[16,1536]{1,0:T(8,128)(2,1)S(1)}, bf16[16,1536]{1,0:T(8,128)(2,1)S(1)}, u32[]{:S(2)}, u32[]{:S(2)}) collective-permute-start(bf16[16,1536]{1,0:T(8,128)(2,1)S(1)} %get-tuple-element.27), channel_id=1, source_target_pairs={{0,4},{1,5},{2,6},{3,7},{4,0},{5,1},{6,2},{7,3},{8,12},{9,13},{10,... | collective-permute-start | bytes 147464 | tf_op jit(solution)/shard_map/ppermute | solution.py:411
  54.4 0.7 %collective-permute-start.15 = (bf16[16,1536]{1,0:T(8,128)(2,1)S(1)}, bf16[16,1536]{1,0:T(8,128)(2,1)S(1)}, u32[]{:S(2)}, u32[]{:S(2)}) collective-permute-start(bf16[16,1536]{1,0:T(8,128)(2,1)S(1)} %get-tuple-element.28), channel_id=1, source_target_pairs={{0,2},{1,3},{2,0},{3,1},{4,6},{5,7},{6,4},{7,5},{8,10},{9,11},{10,... | collective-permute-start | bytes 147464 | tf_op jit(solution)/shard_map/ppermute | solution.py:411
  55.1 1.5 %collective-permute-done.11.refs_2_ = bf16[16,1536]{1,0:T(8,128)(2,1)S(1)} collective-permute-done((bf16[16,1536]{1,0:T(8,128)(2,1)S(1)}, bf16[16,1536]{1,0:T(8,128)(2,1)S(1)}, u32[]{:S(2)}, u32[]{:S(2)}) %collective-permute-start.11) | collective-permute-done | bytes 49184 | tf_op jit(solution)/shard_map/ppermute | solution.py:411
  56.6 1.2 %collective-permute-done.13.refs_4_ = bf16[16,1536]{1,0:T(8,128)(2,1)S(1)} collective-permute-done((bf16[16,1536]{1,0:T(8,128)(2,1)S(1)}, bf16[16,1536]{1,0:T(8,128)(2,1)S(1)}, u32[]{:S(2)}, u32[]{:S(2)}) %collective-permute-start.13) | collective-permute-done | bytes 49184 | tf_op jit(solution)/shard_map/ppermute | solution.py:411
  57.8 0.7 %collective-permute-done.15.refs_6_ = bf16[16,1536]{1,0:T(8,128)(2,1)S(1)} collective-permute-done((bf16[16,1536]{1,0:T(8,128)(2,1)S(1)}, bf16[16,1536]{1,0:T(8,128)(2,1)S(1)}, u32[]{:S(2)}, u32[]{:S(2)}) %collective-permute-start.15) | collective-permute-done | bytes 49184 | tf_op jit(solution)/shard_map/ppermute | solution.py:411
  58.5 0.7 %chip_sum.1 = bf16[16,1536]{1,0:T(8,128)(2,1)} custom-call(f32[16,1536]{1,0:T(8,128)S(1)} %get-tuple-element.21.kept, bf16[16,1536]{1,0:T(8,128)(2,1)S(1)} %collective-permute-done.9.refs_0_, bf16[16,1536]{1,0:T(8,128)(2,1)S(1)} %collective-permute-done.10.refs_1_, bf16[16,1536]{1,0:T(8,128)(2,1)S(1)} %collective-permute-done.11.refs_2_, ...), custom_call_target="tpu_custom_call" | custom-call | tf_op jit(solution)/shard_map/chip_sum/pallas_call | solution.py:357
  (18 shorter events, 0.7 us)
Async XLA Ops:
  4.2 11.3 %collective-permute-start.6 = (bf16[16,1664]{1,0:T(8,128)(2,1)S(1)}, bf16[16,1664]{1,0:T(8,128)(2,1)S(1)}, u32[]{:S(2)}, u32[]{:S(2)}) collective-permute-start(bf16[16,1664]{1,0:T(8,128)(2,1)S(1)} %get-tuple-element.17.payload.refs_0_), channel_id=1, source_target_pairs={{0,14},{1,15},{2,12},{3,13},{4,10},{5,11},{6,8},{7,9},{8,6},{9,7},... | collective-permute-start | bytes 159752 | tf_op jit(solution)/shard_map/ppermute | solution.py:411
  10.2 6.1 %collective-permute-start.5 = (bf16[16,1664]{1,0:T(8,128)(2,1)S(1)}, bf16[16,1664]{1,0:T(8,128)(2,1)S(1)}, u32[]{:S(2)}, u32[]{:S(2)}) collective-permute-start(bf16[16,1664]{1,0:T(8,128)(2,1)S(1)} %get-tuple-element.17.payload.refs_0_), channel_id=1, source_target_pairs={{0,12},{1,13},{2,14},{3,15},{4,8},{5,9},{6,10},{7,11},{8,4},{9,5},... | collective-permute-start | bytes 159752 | tf_op jit(solution)/shard_map/ppermute | solution.py:411
  10.4 9.7 %collective-permute-start.4 = (bf16[16,1664]{1,0:T(8,128)(2,1)S(1)}, bf16[16,1664]{1,0:T(8,128)(2,1)S(1)}, u32[]{:S(2)}, u32[]{:S(2)}) collective-permute-start(bf16[16,1664]{1,0:T(8,128)(2,1)S(1)} %get-tuple-element.17.payload.refs_0_), channel_id=1, source_target_pairs={{0,10},{1,11},{2,8},{3,9},{4,14},{5,15},{6,12},{7,13},{8,2},{9,3},... | collective-permute-start | bytes 159752 | tf_op jit(solution)/shard_map/ppermute | solution.py:411
  11.2 8.9 %collective-permute-start.3 = (bf16[16,1664]{1,0:T(8,128)(2,1)S(1)}, bf16[16,1664]{1,0:T(8,128)(2,1)S(1)}, u32[]{:S(2)}, u32[]{:S(2)}) collective-permute-start(bf16[16,1664]{1,0:T(8,128)(2,1)S(1)} %get-tuple-element.17.payload.refs_0_), channel_id=1, source_target_pairs={{0,8},{1,9},{2,10},{3,11},{4,12},{5,13},{6,14},{7,15},{8,0},{9,1},... | collective-permute-start | bytes 159752 | tf_op jit(solution)/shard_map/ppermute | solution.py:411
  13.2 6.9 %collective-permute-start.2 = (bf16[16,1664]{1,0:T(8,128)(2,1)S(1)}, bf16[16,1664]{1,0:T(8,128)(2,1)S(1)}, u32[]{:S(2)}, u32[]{:S(2)}) collective-permute-start(bf16[16,1664]{1,0:T(8,128)(2,1)S(1)} %get-tuple-element.17.payload.refs_0_), channel_id=1, source_target_pairs={{0,6},{1,7},{2,4},{3,5},{4,2},{5,3},{6,0},{7,1},{8,14},{9,15},{10,... | collective-permute-start | bytes 159752 | tf_op jit(solution)/shard_map/ppermute | solution.py:411
  15.5 4.6 %collective-permute-start.1 = (bf16[16,1664]{1,0:T(8,128)(2,1)S(1)}, bf16[16,1664]{1,0:T(8,128)(2,1)S(1)}, u32[]{:S(2)}, u32[]{:S(2)}) collective-permute-start(bf16[16,1664]{1,0:T(8,128)(2,1)S(1)} %get-tuple-element.17.payload.refs_0_), channel_id=1, source_target_pairs={{0,4},{1,5},{2,6},{3,7},{4,0},{5,1},{6,2},{7,3},{8,12},{9,13},{10,... | collective-permute-start | bytes 159752 | tf_op jit(solution)/shard_map/ppermute | solution.py:411
  16.3 4.1 %collective-permute-start = (bf16[16,1664]{1,0:T(8,128)(2,1)S(1)}, bf16[16,1664]{1,0:T(8,128)(2,1)S(1)}, u32[]{:S(2)}, u32[]{:S(2)}) collective-permute-start(bf16[16,1664]{1,0:T(8,128)(2,1)S(1)} %get-tuple-element.17.payload.refs_0_), channel_id=1, source_target_pairs={{0,2},{1,3},{2,0},{3,1},{4,6},{5,7},{6,4},{7,5},{8,10},{9,11},{10,... | collective-permute-start | bytes 159752 | tf_op jit(solution)/shard_map/ppermute | solution.py:411
  20.4 1.9 %copy-start = (bf16[8,16,1664]{2,1,0:T(8,128)(2,1)}, bf16[8,16,1664]{2,1,0:T(8,128)(2,1)S(1)}, u32[]{:S(2)}) copy-start(bf16[8,16,1664]{2,1,0:T(8,128)(2,1)S(1)} %collect.1.refs_0_) | copy-start | bytes 1277956
  20.5 1.8 %collective-permute-start.7 = (bf16[8,16,1664]{2,1,0:T(8,128)(2,1)S(1)}, bf16[8,16,1664]{2,1,0:T(8,128)(2,1)S(1)}, u32[]{:S(2)}, u32[]{:S(2)}) collective-permute-start(bf16[8,16,1664]{2,1,0:T(8,128)(2,1)S(1)} %collect.1.refs_0_), channel_id=1, source_target_pairs={{0,1},{1,0},{2,3},{3,2},{4,5},{5,4},{6,7},{7,6},{8,9},{9,8},{10,11... | collective-permute-start | bytes 1277960 | tf_op jit(solution)/shard_map/ppermute | solution.py:411
  22.3 0.8 %copy-start.1 = (bf16[8,16,1664]{2,1,0:T(8,128)(2,1)}, bf16[8,16,1664]{2,1,0:T(8,128)(2,1)S(1)}, u32[]{:S(2)}) copy-start(bf16[8,16,1664]{2,1,0:T(8,128)(2,1)S(1)} %collective-permute-done.7.refs_1_) | copy-start | bytes 1277956
  42.0 1.8 %collective-permute-start.8 = (bf16[2,64,1536]{2,1,0:T(8,128)(2,1)S(1)}, bf16[2,64,1536]{2,1,0:T(8,128)(2,1)S(1)}, u32[]{:S(2)}, u32[]{:S(2)}) collective-permute-start(bf16[2,64,1536]{2,1,0:T(8,128)(2,1)S(1)} %get-tuple-element.20), channel_id=1, source_target_pairs={{0,1},{1,0},{2,3},{3,2},{4,5},{5,4},{6,7},{7,6},{8,9},{9,8},{10,11... | collective-permute-start | bytes 1179656 | tf_op jit(solution)/shard_map/ppermute | solution.py:411
  43.9 9.7 %collective-permute-start.9 = (bf16[16,1536]{1,0:T(8,128)(2,1)S(1)}, bf16[16,1536]{1,0:T(8,128)(2,1)S(1)}, u32[]{:S(2)}, u32[]{:S(2)}) collective-permute-start(bf16[16,1536]{1,0:T(8,128)(2,1)S(1)} %get-tuple-element.22), channel_id=1, source_target_pairs={{0,14},{1,15},{2,12},{3,13},{4,10},{5,11},{6,8},{7,9},{8,6},{9,7},... | collective-permute-start | bytes 147464 | tf_op jit(solution)/shard_map/ppermute | solution.py:411
  48.3 6.1 %collective-permute-start.10 = (bf16[16,1536]{1,0:T(8,128)(2,1)S(1)}, bf16[16,1536]{1,0:T(8,128)(2,1)S(1)}, u32[]{:S(2)}, u32[]{:S(2)}) collective-permute-start(bf16[16,1536]{1,0:T(8,128)(2,1)S(1)} %get-tuple-element.23), channel_id=1, source_target_pairs={{0,12},{1,13},{2,14},{3,15},{4,8},{5,9},{6,10},{7,11},{8,4},{9,5},... | collective-permute-start | bytes 147464 | tf_op jit(solution)/shard_map/ppermute | solution.py:411
  48.5 8.1 %collective-permute-start.11 = (bf16[16,1536]{1,0:T(8,128)(2,1)S(1)}, bf16[16,1536]{1,0:T(8,128)(2,1)S(1)}, u32[]{:S(2)}, u32[]{:S(2)}) collective-permute-start(bf16[16,1536]{1,0:T(8,128)(2,1)S(1)} %get-tuple-element.24), channel_id=1, source_target_pairs={{0,10},{1,11},{2,8},{3,9},{4,14},{5,15},{6,12},{7,13},{8,2},{9,3},... | collective-permute-start | bytes 147464 | tf_op jit(solution)/shard_map/ppermute | solution.py:411
  49.2 7.4 %collective-permute-start.12 = (bf16[16,1536]{1,0:T(8,128)(2,1)S(1)}, bf16[16,1536]{1,0:T(8,128)(2,1)S(1)}, u32[]{:S(2)}, u32[]{:S(2)}) collective-permute-start(bf16[16,1536]{1,0:T(8,128)(2,1)S(1)} %get-tuple-element.25), channel_id=1, source_target_pairs={{0,8},{1,9},{2,10},{3,11},{4,12},{5,13},{6,14},{7,15},{8,0},{9,1},... | collective-permute-start | bytes 147464 | tf_op jit(solution)/shard_map/ppermute | solution.py:411
  51.6 6.2 %collective-permute-start.13 = (bf16[16,1536]{1,0:T(8,128)(2,1)S(1)}, bf16[16,1536]{1,0:T(8,128)(2,1)S(1)}, u32[]{:S(2)}, u32[]{:S(2)}) collective-permute-start(bf16[16,1536]{1,0:T(8,128)(2,1)S(1)} %get-tuple-element.26), channel_id=1, source_target_pairs={{0,6},{1,7},{2,4},{3,5},{4,2},{5,3},{6,0},{7,1},{8,14},{9,15},{10,... | collective-permute-start | bytes 147464 | tf_op jit(solution)/shard_map/ppermute | solution.py:411
  53.6 4.2 %collective-permute-start.14 = (bf16[16,1536]{1,0:T(8,128)(2,1)S(1)}, bf16[16,1536]{1,0:T(8,128)(2,1)S(1)}, u32[]{:S(2)}, u32[]{:S(2)}) collective-permute-start(bf16[16,1536]{1,0:T(8,128)(2,1)S(1)} %get-tuple-element.27), channel_id=1, source_target_pairs={{0,4},{1,5},{2,6},{3,7},{4,0},{5,1},{6,2},{7,3},{8,12},{9,13},{10,... | collective-permute-start | bytes 147464 | tf_op jit(solution)/shard_map/ppermute | solution.py:411
  54.4 4.1 %collective-permute-start.15 = (bf16[16,1536]{1,0:T(8,128)(2,1)S(1)}, bf16[16,1536]{1,0:T(8,128)(2,1)S(1)}, u32[]{:S(2)}, u32[]{:S(2)}) collective-permute-start(bf16[16,1536]{1,0:T(8,128)(2,1)S(1)} %get-tuple-element.28), channel_id=1, source_target_pairs={{0,2},{1,3},{2,0},{3,1},{4,6},{5,7},{6,4},{7,5},{8,10},{9,11},{10,... | collective-permute-start | bytes 147464 | tf_op jit(solution)/shard_map/ppermute | solution.py:411

commit v5 on v4

--- a/solution.py
+++ b/solution.py
@@ -306,15 +306,14 @@
         + in_vmem(len(pieces) + len(early)),
         out_specs=in_vmem(n_out),
         scratch_shapes=scratch,
-        compiler_params=pltpu.CompilerParams(vmem_limit_bytes=38 * MIB),
+        compiler_params=pltpu.CompilerParams(vmem_limit_bytes=73 * MIB // 2),
         name="experts",
     )(
         placement,
         router,
         from_hbm(w_up),
         from_hbm(w_down),
-        *pieces,
-        *[pltpu.with_memory_space_constraint(e, VMEM) for e in early],
+        *[pltpu.with_memory_space_constraint(a, VMEM) for a in [*pieces, *early]],
     )
 
 

time: 59.3 us -> 58.3 us (0.983)
  local copies, waits for them, and re-layouts: 0.75 us -> 0 us
    unnamed x4 -> x0, local copies, waits for them, and re-layouts: 0.75 us -> none
where the time goes in v5:
time: 58.3 us; the launch traced here: 58.1 us
  Pallas kernels  26.9 us (46%)
  starting transfers between devices  24 us (41%)
  waiting for transfers between devices  7.04 us (12%)
    ppermute x16, starting transfers between devices, swap(): return lax.ppermute(value, ('ae', 'tp', 'sub'), pairs)  24 us
    pallas_call x1, Pallas kernels, run_experts(): pl.pallas_call(functools.partial(expert_kernel, plan, len(early), n_out),...  18.7 us
    ppermute x16, waiting for transfers between devices, swap(): return lax.ppermute(value, ('ae', 'tp', 'sub'), pairs)  7.04 us
    pallas_call x1, Pallas kernels, attend(): pl.pallas_call(functools.partial(attention_kernel, n_early), out_shape=ou...  4.15 us
    pallas_call x1, Pallas kernels, stage(): pl.pallas_call(functools.partial(stage_kernel, start), out_shape=VMEM((co...  3.35 us
  transfers between devices with their start and end apart: 16, of which 7 were waited for; matrix products, arithmetic and copies ran while one was open for 0% of the time, Pallas kernels for 6%

profile of v5, /device:TPU:0, one launch (start us, length us, event | category | flops | bytes accessed | tf_op | source)
XLA Modules:
  0.0 58.1 jit_solution(1957527742491494397)
XLA Ops:
  0.0 4.1 %attention.1 = (bf16[16,1664]{1,0:T(8,128)(2,1)S(1)}, bf16[1344,3072]{1,0:T(8,128)(2,1)S(1)}) custom-call(bf16[2,16,4,64,128]{4,3,2,1,0:T(8,128)(2,1)} %refs_0_.1, bf16[16,1536]{1,0:T(8,128)(2,1)} %refs_1_.1, bf16[2,16,512]{2,1,0:T(8,128)(2,1)} %refs_2_.1, bf16[16,1536]{1,0:T(8,128)(2,1)} %refs_3_.1, s32[1,16]{1,0:T(1,128)} %bitcast.13, s32[4,16]{1,0:T(4,128)} %bitcast.12, ...), custom_call_target="tpu_custom_call" | custom-call | tf_op jit(solution)/shard_map/attention/pallas_call | solution.py:122
  4.2 6.0 %collective-permute-start.6 = (bf16[16,1664]{1,0:T(8,128)(2,1)S(1)}, bf16[16,1664]{1,0:T(8,128)(2,1)S(1)}, u32[]{:S(2)}, u32[]{:S(2)}) collective-permute-start(bf16[16,1664]{1,0:T(8,128)(2,1)S(1)} %get-tuple-element.17.payload.refs_0_), channel_id=1, source_target_pairs={{0,14},{1,15},{2,12},{3,13},{4,10},{5,11},{6,8},{7,9},{8,6},{9,7},... | collective-permute-start | bytes 159752 | tf_op jit(solution)/shard_map/ppermute | solution.py:410
  10.2 0.2 collective-permute-start.5
  10.4 0.8 %collective-permute-start.4 = (bf16[16,1664]{1,0:T(8,128)(2,1)S(1)}, bf16[16,1664]{1,0:T(8,128)(2,1)S(1)}, u32[]{:S(2)}, u32[]{:S(2)}) collective-permute-start(bf16[16,1664]{1,0:T(8,128)(2,1)S(1)} %get-tuple-element.17.payload.refs_0_), channel_id=1, source_target_pairs={{0,10},{1,11},{2,8},{3,9},{4,14},{5,15},{6,12},{7,13},{8,2},{9,3},... | collective-permute-start | bytes 159752 | tf_op jit(solution)/shard_map/ppermute | solution.py:410
  11.2 2.0 %collective-permute-start.3 = (bf16[16,1664]{1,0:T(8,128)(2,1)S(1)}, bf16[16,1664]{1,0:T(8,128)(2,1)S(1)}, u32[]{:S(2)}, u32[]{:S(2)}) collective-permute-start(bf16[16,1664]{1,0:T(8,128)(2,1)S(1)} %get-tuple-element.17.payload.refs_0_), channel_id=1, source_target_pairs={{0,8},{1,9},{2,10},{3,11},{4,12},{5,13},{6,14},{7,15},{8,0},{9,1},... | collective-permute-start | bytes 159752 | tf_op jit(solution)/shard_map/ppermute | solution.py:410
  13.2 2.3 %collective-permute-start.2 = (bf16[16,1664]{1,0:T(8,128)(2,1)S(1)}, bf16[16,1664]{1,0:T(8,128)(2,1)S(1)}, u32[]{:S(2)}, u32[]{:S(2)}) collective-permute-start(bf16[16,1664]{1,0:T(8,128)(2,1)S(1)} %get-tuple-element.17.payload.refs_0_), channel_id=1, source_target_pairs={{0,6},{1,7},{2,4},{3,5},{4,2},{5,3},{6,0},{7,1},{8,14},{9,15},{10,... | collective-permute-start | bytes 159752 | tf_op jit(solution)/shard_map/ppermute | solution.py:410
  15.5 0.8 %collective-permute-start.1 = (bf16[16,1664]{1,0:T(8,128)(2,1)S(1)}, bf16[16,1664]{1,0:T(8,128)(2,1)S(1)}, u32[]{:S(2)}, u32[]{:S(2)}) collective-permute-start(bf16[16,1664]{1,0:T(8,128)(2,1)S(1)} %get-tuple-element.17.payload.refs_0_), channel_id=1, source_target_pairs={{0,4},{1,5},{2,6},{3,7},{4,0},{5,1},{6,2},{7,3},{8,12},{9,13},{10,... | collective-permute-start | bytes 159752 | tf_op jit(solution)/shard_map/ppermute | solution.py:410
  16.3 0.4 collective-permute-start
  16.7 3.4 %stage.1.staged.refs_3_ = bf16[1344,3072]{1,0:T(8,128)(2,1)S(1)} custom-call(bf16[5376,3072]{1,0:T(8,128)(2,1)} %bitcast.8, bf16[16,1664]{1,0:T(8,128)(2,1)S(1)} %get-tuple-element.17.payload.refs_0_), custom_call_target="tpu_custom_call" | custom-call | bytes 16515072 | tf_op jit(solution)/shard_map/stage/pallas_call | solution.py:146
  20.1 0.3 collective-permute-done.refs_1_
  20.5 1.8 %collective-permute-done.7.refs_1_ = bf16[8,16,1664]{2,1,0:T(8,128)(2,1)S(1)} collective-permute-done((bf16[8,16,1664]{2,1,0:T(8,128)(2,1)S(1)}, bf16[8,16,1664]{2,1,0:T(8,128)(2,1)S(1)}, u32[]{:S(2)}, u32[]{:S(2)}) %collective-permute-start.7) | collective-permute-done | bytes 426016 | tf_op jit(solution)/shard_map/ppermute | solution.py:410
  22.3 18.7 %experts.1 = (f32[2,64,1536]{2,1,0:T(8,128)S(1)}, bf16[2,64,1536]{2,1,0:T(8,128)(2,1)S(1)}) custom-call(s32[16]{0:T(128)} %placement.1, bf16[16,3072]{1,0:T(8,128)(2,1)} %bitcast.11, bf16[5376,3072]{1,0:T(8,128)(2,1)} %bitcast.9, bf16[5376,3072]{1,0:T(8,128)(2,1)} %bitcast.10, bf16[8,16,1664]{2,1,0:T(8,128)(2,1)S(1)} %collect.1.refs_0_, ...), custom_call_target="tpu_custom_call" | custom-call | tf_op jit(solution)/shard_map/experts/pallas_call | solution.py:300
  41.2 1.6 %collective-permute-done.8.other = bf16[2,64,1536]{2,1,0:T(8,128)(2,1)S(1)} collective-permute-done((bf16[2,64,1536]{2,1,0:T(8,128)(2,1)S(1)}, bf16[2,64,1536]{2,1,0:T(8,128)(2,1)S(1)}, u32[]{:S(2)}, u32[]{:S(2)}) %collective-permute-start.8) | collective-permute-done | bytes 393248 | tf_op jit(solution)/shard_map/ppermute | solution.py:410
  42.8 4.4 %collective-permute-start.9 = (bf16[16,1536]{1,0:T(8,128)(2,1)S(1)}, bf16[16,1536]{1,0:T(8,128)(2,1)S(1)}, u32[]{:S(2)}, u32[]{:S(2)}) collective-permute-start(bf16[16,1536]{1,0:T(8,128)(2,1)S(1)} %get-tuple-element.22), channel_id=1, source_target_pairs={{0,14},{1,15},{2,12},{3,13},{4,10},{5,11},{6,8},{7,9},{8,6},{9,7},... | collective-permute-start | bytes 147464 | tf_op jit(solution)/shard_map/ppermute | solution.py:410
  47.2 0.2 collective-permute-start.10
  47.5 0.7 %collective-permute-start.11 = (bf16[16,1536]{1,0:T(8,128)(2,1)S(1)}, bf16[16,1536]{1,0:T(8,128)(2,1)S(1)}, u32[]{:S(2)}, u32[]{:S(2)}) collective-permute-start(bf16[16,1536]{1,0:T(8,128)(2,1)S(1)} %get-tuple-element.24), channel_id=1, source_target_pairs={{0,10},{1,11},{2,8},{3,9},{4,14},{5,15},{6,12},{7,13},{8,2},{9,3},... | collective-permute-start | bytes 147464 | tf_op jit(solution)/shard_map/ppermute | solution.py:410
  48.2 2.3 %collective-permute-start.12 = (bf16[16,1536]{1,0:T(8,128)(2,1)S(1)}, bf16[16,1536]{1,0:T(8,128)(2,1)S(1)}, u32[]{:S(2)}, u32[]{:S(2)}) collective-permute-start(bf16[16,1536]{1,0:T(8,128)(2,1)S(1)} %get-tuple-element.25), channel_id=1, source_target_pairs={{0,8},{1,9},{2,10},{3,11},{4,12},{5,13},{6,14},{7,15},{8,0},{9,1},... | collective-permute-start | bytes 147464 | tf_op jit(solution)/shard_map/ppermute | solution.py:410
  50.5 2.0 %collective-permute-start.13 = (bf16[16,1536]{1,0:T(8,128)(2,1)S(1)}, bf16[16,1536]{1,0:T(8,128)(2,1)S(1)}, u32[]{:S(2)}, u32[]{:S(2)}) collective-permute-start(bf16[16,1536]{1,0:T(8,128)(2,1)S(1)} %get-tuple-element.26), channel_id=1, source_target_pairs={{0,6},{1,7},{2,4},{3,5},{4,2},{5,3},{6,0},{7,1},{8,14},{9,15},{10,... | collective-permute-start | bytes 147464 | tf_op jit(solution)/shard_map/ppermute | solution.py:410
  52.5 0.8 %collective-permute-start.14 = (bf16[16,1536]{1,0:T(8,128)(2,1)S(1)}, bf16[16,1536]{1,0:T(8,128)(2,1)S(1)}, u32[]{:S(2)}, u32[]{:S(2)}) collective-permute-start(bf16[16,1536]{1,0:T(8,128)(2,1)S(1)} %get-tuple-element.27), channel_id=1, source_target_pairs={{0,4},{1,5},{2,6},{3,7},{4,0},{5,1},{6,2},{7,3},{8,12},{9,13},{10,... | collective-permute-start | bytes 147464 | tf_op jit(solution)/shard_map/ppermute | solution.py:410
  53.3 0.7 %collective-permute-start.15 = (bf16[16,1536]{1,0:T(8,128)(2,1)S(1)}, bf16[16,1536]{1,0:T(8,128)(2,1)S(1)}, u32[]{:S(2)}, u32[]{:S(2)}) collective-permute-start(bf16[16,1536]{1,0:T(8,128)(2,1)S(1)} %get-tuple-element.28), channel_id=1, source_target_pairs={{0,2},{1,3},{2,0},{3,1},{4,6},{5,7},{6,4},{7,5},{8,10},{9,11},{10,... | collective-permute-start | bytes 147464 | tf_op jit(solution)/shard_map/ppermute | solution.py:410
  54.0 1.5 %collective-permute-done.11.refs_2_ = bf16[16,1536]{1,0:T(8,128)(2,1)S(1)} collective-permute-done((bf16[16,1536]{1,0:T(8,128)(2,1)S(1)}, bf16[16,1536]{1,0:T(8,128)(2,1)S(1)}, u32[]{:S(2)}, u32[]{:S(2)}) %collective-permute-start.11) | collective-permute-done | bytes 49184 | tf_op jit(solution)/shard_map/ppermute | solution.py:410
  55.6 1.2 %collective-permute-done.13.refs_4_ = bf16[16,1536]{1,0:T(8,128)(2,1)S(1)} collective-permute-done((bf16[16,1536]{1,0:T(8,128)(2,1)S(1)}, bf16[16,1536]{1,0:T(8,128)(2,1)S(1)}, u32[]{:S(2)}, u32[]{:S(2)}) %collective-permute-start.13) | collective-permute-done | bytes 49184 | tf_op jit(solution)/shard_map/ppermute | solution.py:410
  56.8 0.6 %collective-permute-done.15.refs_6_ = bf16[16,1536]{1,0:T(8,128)(2,1)S(1)} collective-permute-done((bf16[16,1536]{1,0:T(8,128)(2,1)S(1)}, bf16[16,1536]{1,0:T(8,128)(2,1)S(1)}, u32[]{:S(2)}, u32[]{:S(2)}) %collective-permute-start.15) | collective-permute-done | bytes 49184 | tf_op jit(solution)/shard_map/ppermute | solution.py:410
  57.4 0.7 %chip_sum.1 = bf16[16,1536]{1,0:T(8,128)(2,1)} custom-call(f32[16,1536]{1,0:T(8,128)S(1)} %get-tuple-element.21.kept, bf16[16,1536]{1,0:T(8,128)(2,1)S(1)} %collective-permute-done.9.refs_0_, bf16[16,1536]{1,0:T(8,128)(2,1)S(1)} %collective-permute-done.10.refs_1_, bf16[16,1536]{1,0:T(8,128)(2,1)S(1)} %collective-permute-done.11.refs_2_, ...), custom_call_target="tpu_custom_call" | custom-call | tf_op jit(solution)/shard_map/chip_sum/pallas_call | solution.py:356
  (14 shorter events, 0.5 us)
Async XLA Ops:
  4.2 11.3 %collective-permute-start.6 = (bf16[16,1664]{1,0:T(8,128)(2,1)S(1)}, bf16[16,1664]{1,0:T(8,128)(2,1)S(1)}, u32[]{:S(2)}, u32[]{:S(2)}) collective-permute-start(bf16[16,1664]{1,0:T(8,128)(2,1)S(1)} %get-tuple-element.17.payload.refs_0_), channel_id=1, source_target_pairs={{0,14},{1,15},{2,12},{3,13},{4,10},{5,11},{6,8},{7,9},{8,6},{9,7},... | collective-permute-start | bytes 159752 | tf_op jit(solution)/shard_map/ppermute | solution.py:410
  10.2 6.1 %collective-permute-start.5 = (bf16[16,1664]{1,0:T(8,128)(2,1)S(1)}, bf16[16,1664]{1,0:T(8,128)(2,1)S(1)}, u32[]{:S(2)}, u32[]{:S(2)}) collective-permute-start(bf16[16,1664]{1,0:T(8,128)(2,1)S(1)} %get-tuple-element.17.payload.refs_0_), channel_id=1, source_target_pairs={{0,12},{1,13},{2,14},{3,15},{4,8},{5,9},{6,10},{7,11},{8,4},{9,5},... | collective-permute-start | bytes 159752 | tf_op jit(solution)/shard_map/ppermute | solution.py:410
  10.4 9.7 %collective-permute-start.4 = (bf16[16,1664]{1,0:T(8,128)(2,1)S(1)}, bf16[16,1664]{1,0:T(8,128)(2,1)S(1)}, u32[]{:S(2)}, u32[]{:S(2)}) collective-permute-start(bf16[16,1664]{1,0:T(8,128)(2,1)S(1)} %get-tuple-element.17.payload.refs_0_), channel_id=1, source_target_pairs={{0,10},{1,11},{2,8},{3,9},{4,14},{5,15},{6,12},{7,13},{8,2},{9,3},... | collective-permute-start | bytes 159752 | tf_op jit(solution)/shard_map/ppermute | solution.py:410
  11.2 8.9 %collective-permute-start.3 = (bf16[16,1664]{1,0:T(8,128)(2,1)S(1)}, bf16[16,1664]{1,0:T(8,128)(2,1)S(1)}, u32[]{:S(2)}, u32[]{:S(2)}) collective-permute-start(bf16[16,1664]{1,0:T(8,128)(2,1)S(1)} %get-tuple-element.17.payload.refs_0_), channel_id=1, source_target_pairs={{0,8},{1,9},{2,10},{3,11},{4,12},{5,13},{6,14},{7,15},{8,0},{9,1},... | collective-permute-start | bytes 159752 | tf_op jit(solution)/shard_map/ppermute | solution.py:410
  13.2 6.9 %collective-permute-start.2 = (bf16[16,1664]{1,0:T(8,128)(2,1)S(1)}, bf16[16,1664]{1,0:T(8,128)(2,1)S(1)}, u32[]{:S(2)}, u32[]{:S(2)}) collective-permute-start(bf16[16,1664]{1,0:T(8,128)(2,1)S(1)} %get-tuple-element.17.payload.refs_0_), channel_id=1, source_target_pairs={{0,6},{1,7},{2,4},{3,5},{4,2},{5,3},{6,0},{7,1},{8,14},{9,15},{10,... | collective-permute-start | bytes 159752 | tf_op jit(solution)/shard_map/ppermute | solution.py:410
  15.5 4.6 %collective-permute-start.1 = (bf16[16,1664]{1,0:T(8,128)(2,1)S(1)}, bf16[16,1664]{1,0:T(8,128)(2,1)S(1)}, u32[]{:S(2)}, u32[]{:S(2)}) collective-permute-start(bf16[16,1664]{1,0:T(8,128)(2,1)S(1)} %get-tuple-element.17.payload.refs_0_), channel_id=1, source_target_pairs={{0,4},{1,5},{2,6},{3,7},{4,0},{5,1},{6,2},{7,3},{8,12},{9,13},{10,... | collective-permute-start | bytes 159752 | tf_op jit(solution)/shard_map/ppermute | solution.py:410
  16.3 4.1 %collective-permute-start = (bf16[16,1664]{1,0:T(8,128)(2,1)S(1)}, bf16[16,1664]{1,0:T(8,128)(2,1)S(1)}, u32[]{:S(2)}, u32[]{:S(2)}) collective-permute-start(bf16[16,1664]{1,0:T(8,128)(2,1)S(1)} %get-tuple-element.17.payload.refs_0_), channel_id=1, source_target_pairs={{0,2},{1,3},{2,0},{3,1},{4,6},{5,7},{6,4},{7,5},{8,10},{9,11},{10,... | collective-permute-start | bytes 159752 | tf_op jit(solution)/shard_map/ppermute | solution.py:410
  20.4 1.8 %collective-permute-start.7 = (bf16[8,16,1664]{2,1,0:T(8,128)(2,1)S(1)}, bf16[8,16,1664]{2,1,0:T(8,128)(2,1)S(1)}, u32[]{:S(2)}, u32[]{:S(2)}) collective-permute-start(bf16[8,16,1664]{2,1,0:T(8,128)(2,1)S(1)} %collect.1.refs_0_), channel_id=1, source_target_pairs={{0,1},{1,0},{2,3},{3,2},{4,5},{5,4},{6,7},{7,6},{8,9},{9,8},{10,11... | collective-permute-start | bytes 1277960 | tf_op jit(solution)/shard_map/ppermute | solution.py:410
  41.0 1.8 %collective-permute-start.8 = (bf16[2,64,1536]{2,1,0:T(8,128)(2,1)S(1)}, bf16[2,64,1536]{2,1,0:T(8,128)(2,1)S(1)}, u32[]{:S(2)}, u32[]{:S(2)}) collective-permute-start(bf16[2,64,1536]{2,1,0:T(8,128)(2,1)S(1)} %get-tuple-element.20), channel_id=1, source_target_pairs={{0,1},{1,0},{2,3},{3,2},{4,5},{5,4},{6,7},{7,6},{8,9},{9,8},{10,11... | collective-permute-start | bytes 1179656 | tf_op jit(solution)/shard_map/ppermute | solution.py:410
  42.8 9.7 %collective-permute-start.9 = (bf16[16,1536]{1,0:T(8,128)(2,1)S(1)}, bf16[16,1536]{1,0:T(8,128)(2,1)S(1)}, u32[]{:S(2)}, u32[]{:S(2)}) collective-permute-start(bf16[16,1536]{1,0:T(8,128)(2,1)S(1)} %get-tuple-element.22), channel_id=1, source_target_pairs={{0,14},{1,15},{2,12},{3,13},{4,10},{5,11},{6,8},{7,9},{8,6},{9,7},... | collective-permute-start | bytes 147464 | tf_op jit(solution)/shard_map/ppermute | solution.py:410
  47.2 6.1 %collective-permute-start.10 = (bf16[16,1536]{1,0:T(8,128)(2,1)S(1)}, bf16[16,1536]{1,0:T(8,128)(2,1)S(1)}, u32[]{:S(2)}, u32[]{:S(2)}) collective-permute-start(bf16[16,1536]{1,0:T(8,128)(2,1)S(1)} %get-tuple-element.23), channel_id=1, source_target_pairs={{0,12},{1,13},{2,14},{3,15},{4,8},{5,9},{6,10},{7,11},{8,4},{9,5},... | collective-permute-start | bytes 147464 | tf_op jit(solution)/shard_map/ppermute | solution.py:410
  47.5 8.1 %collective-permute-start.11 = (bf16[16,1536]{1,0:T(8,128)(2,1)S(1)}, bf16[16,1536]{1,0:T(8,128)(2,1)S(1)}, u32[]{:S(2)}, u32[]{:S(2)}) collective-permute-start(bf16[16,1536]{1,0:T(8,128)(2,1)S(1)} %get-tuple-element.24), channel_id=1, source_target_pairs={{0,10},{1,11},{2,8},{3,9},{4,14},{5,15},{6,12},{7,13},{8,2},{9,3},... | collective-permute-start | bytes 147464 | tf_op jit(solution)/shard_map/ppermute | solution.py:410
  48.2 7.4 %collective-permute-start.12 = (bf16[16,1536]{1,0:T(8,128)(2,1)S(1)}, bf16[16,1536]{1,0:T(8,128)(2,1)S(1)}, u32[]{:S(2)}, u32[]{:S(2)}) collective-permute-start(bf16[16,1536]{1,0:T(8,128)(2,1)S(1)} %get-tuple-element.25), channel_id=1, source_target_pairs={{0,8},{1,9},{2,10},{3,11},{4,12},{5,13},{6,14},{7,15},{8,0},{9,1},... | collective-permute-start | bytes 147464 | tf_op jit(solution)/shard_map/ppermute | solution.py:410
  50.5 6.2 %collective-permute-start.13 = (bf16[16,1536]{1,0:T(8,128)(2,1)S(1)}, bf16[16,1536]{1,0:T(8,128)(2,1)S(1)}, u32[]{:S(2)}, u32[]{:S(2)}) collective-permute-start(bf16[16,1536]{1,0:T(8,128)(2,1)S(1)} %get-tuple-element.26), channel_id=1, source_target_pairs={{0,6},{1,7},{2,4},{3,5},{4,2},{5,3},{6,0},{7,1},{8,14},{9,15},{10,... | collective-permute-start | bytes 147464 | tf_op jit(solution)/shard_map/ppermute | solution.py:410
  52.5 4.2 %collective-permute-start.14 = (bf16[16,1536]{1,0:T(8,128)(2,1)S(1)}, bf16[16,1536]{1,0:T(8,128)(2,1)S(1)}, u32[]{:S(2)}, u32[]{:S(2)}) collective-permute-start(bf16[16,1536]{1,0:T(8,128)(2,1)S(1)} %get-tuple-element.27), channel_id=1, source_target_pairs={{0,4},{1,5},{2,6},{3,7},{4,0},{5,1},{6,2},{7,3},{8,12},{9,13},{10,... | collective-permute-start | bytes 147464 | tf_op jit(solution)/shard_map/ppermute | solution.py:410
  53.3 4.1 %collective-permute-start.15 = (bf16[16,1536]{1,0:T(8,128)(2,1)S(1)}, bf16[16,1536]{1,0:T(8,128)(2,1)S(1)}, u32[]{:S(2)}, u32[]{:S(2)}) collective-permute-start(bf16[16,1536]{1,0:T(8,128)(2,1)S(1)} %get-tuple-element.28), channel_id=1, source_target_pairs={{0,2},{1,3},{2,0},{3,1},{4,6},{5,7},{6,4},{7,5},{8,10},{9,11},{10,... | collective-permute-start | bytes 147464 | tf_op jit(solution)/shard_map/ppermute | solution.py:410
